TPU v7x, 128 devices: a whole 4x4x4 slice. The times are simulated.
128 devices in a mesh: row: 4 (over x), col: 16 (over z, y), depth: 2 (over core).
Axes of the slice: x: 4, y: 4, z: 4, core: 2. Of those that a mesh axis runs over, the one named last changes fastest.
Arguments:
- density: float32 [4096, 4096], P('row', 'col'), as said below
- pattern: int32 [64, 64], P('row', 'col'), may hold values from 0 to 1, as said below
- branches: int32 [3], replicated, may hold values from 0 to 1, as said below
Outputs:
- purified: float32 [4096, 4096], P('row', 'col')
- traces: float32 [3], replicated
Inputs may be any that keep to these rules, and one draw needn't show every extreme that they name: `pattern`: symmetric, and every diagonal block is 1. `density`: symmetric, and zero in every block where pattern is 0. `branches`: the first step's value differs from the last step's.
All inputs are finite; a program needn't handle non-finite values.
Results may differ from a plain program's by a relative error of at most 0.00015.
Values sent between devices are 32-bit elements; how exact they have to be, the bound alone decides.
A program may use at most 64 MiB of HBM per device.

v0:
```python
import jax
import jax.numpy as jnp
from jax import lax
from jax.sharding import PartitionSpec as P

BS = 64
STEPS = 3


def pick_blocks(values_tile, along, depth_slot, depth_count, block_size):
    height, breadth = values_tile.shape
    if along == 0:
        blocks = values_tile.reshape(
            height // (depth_count * block_size), depth_count, block_size, breadth
        )
        blocks = lax.dynamic_slice_in_dim(blocks, depth_slot, 1, 1)
        return blocks.reshape(height // depth_count, breadth)
    blocks = values_tile.reshape(
        height, breadth // (depth_count * block_size), depth_count, block_size
    )
    blocks = lax.dynamic_slice_in_dim(blocks, depth_slot, 1, 2)
    return blocks.reshape(height, breadth // depth_count)


def apply_pattern(values_tile, kept_blocks):
    block_rows, block_cols = kept_blocks.shape
    height, breadth = values_tile.shape
    shaped = values_tile.reshape(
        block_rows, height // block_rows, block_cols, breadth // block_cols
    )
    return (shaped * kept_blocks.astype(jnp.float32)[:, None, :, None]).reshape(height, breadth)


def diagonal_sum(values_tile, row_ids, col_ids):
    return jnp.sum(jnp.where(row_ids[:, None] == col_ids[None, :], values_tile, 0.0))


def full_product(left_part, right_part):
    return jnp.dot(
        left_part, right_part, precision=lax.Precision.HIGHEST, preferred_element_type=jnp.float32
    )


def per_device(density, pattern, branches):
    rows_t, cols_t = density.shape
    depth_count = lax.axis_size("depth")
    depth_slot = lax.axis_index("depth")
    row_base = lax.axis_index("row") * rows_t
    col_ids = lax.axis_index("col") * cols_t + jnp.arange(cols_t, dtype=jnp.int32)
    share_rows = rows_t // depth_count
    offset_rows = depth_slot * share_rows
    current = density
    local_traces = []
    for section in range(STEPS):
        weight = branches[section].astype(jnp.float32)
        left_piece = pick_blocks(current, 1, depth_slot, depth_count, BS)
        right_piece = pick_blocks(current, 0, depth_slot, depth_count, BS)
        column_panel = lax.all_gather(right_piece, "row", axis=0, tiled=True)
        partial_value = full_product(
            lax.all_gather(left_piece, "col", axis=1, tiled=True), column_panel
        )
        square = lax.psum(partial_value, "depth")
        share_ids = row_base + offset_rows + jnp.arange(share_rows, dtype=jnp.int32)
        square_share = lax.dynamic_slice_in_dim(square, offset_rows, share_rows, 0)
        local_traces.append(diagonal_sum(square_share, share_ids, col_ids))
        current = apply_pattern(square + 2.0 * weight * (current - square), pattern)
    stacked = jnp.stack(local_traces)
    traces = lax.psum(stacked, ("row", "col", "depth"))
    return (current, traces)


def solution(mesh):
    in_specs = (P("row", "col"), P("row", "col"), P())
    out_specs = (P("row", "col"), P())
    return jax.shard_map(
        per_device, mesh=mesh, in_specs=in_specs, out_specs=out_specs, check_vma=False
    )
```

profile of v0, /device:TPU:37, one launch (start us, length us, event | category | flops | bytes accessed | tf_op | source)
XLA Modules:
  0.0 536.2 jit_solution(4092007080639796049)
XLA Ops:
  7.2 2.0 constant_dynamic-slice_fusion.2
  9.3 0.3 copy.8
  9.6 0.8 constant_dynamic-slice_fusion.3
  10.5 30.7 %all-gather.9.cloned.1.call-done = f32[2048,256]{1,0:T(8,128)} async-done(((f32[512,256]{1,0:T(8,128)}), f32[2048,256]{1,0:T(8,128)}) %all-gather.9.cloned.1.call-update) | async-done | bytes 2097168 | tf_op jit(solution)/shard_map/all_gather | solution.py:58
  41.3 74.7 %all-gather.7.cloned.1.call-done = f32[1024,2048]{0,1:T(8,128)} async-done(((f32[1024,128]{0,1:T(8,128)}), f32[1024,2048]{0,1:T(8,128)}) %all-gather.7.cloned.1.call-update) | async-done | bytes 8388624 | tf_op jit(solution)/shard_map/all_gather | solution.py:60
  115.9 17.0 %fusion.4 = f32[1024,256]{1,0:T(8,128)} fusion(f32[1024,2048]{0,1:T(8,128)} %all-gather.7.cloned.1.call-done, f32[2048,256]{1,0:T(8,128)} %all-gather.9.cloned.1.call-done), kind=kOutput, calls=%fused_computation.21 | convolution fusion | flops 6442450944 | bytes 11534336 | tf_op jit(solution)/shard_map/dot_general | solution.py:39
  133.0 0.6 fusion.3
  134.6 24.0 %all-reduce.4.cloned.1.call-done = f32[1024,256]{1,0:T(8,128)} async-done(((f32[1024,256]{1,0:T(8,128)}), f32[1024,256]{1,0:T(8,128)}) %all-reduce.4.cloned.1.call-update) | async-done | bytes 1048592 | tf_op jit(solution)/shard_map/psum | solution.py:62
  158.6 1.4 multiply_add_fusion.1
  159.9 0.8 dynamic-slice_multiply_fusion.2
  161.1 0.3 copy.9
  161.4 0.8 dynamic-slice_multiply_fusion.3
  162.3 0.2 all-reduce.6.cloned.1.call-start
  162.5 28.9 %all-gather.13.cloned.1.call-done = f32[2048,256]{1,0:T(8,128)} async-done(((f32[512,256]{1,0:T(8,128)}), f32[2048,256]{1,0:T(8,128)}) %all-gather.13.cloned.1.call-update) | async-done | bytes 2097168 | tf_op jit(solution)/shard_map/all_gather | solution.py:58
  191.4 74.7 %all-gather.11.cloned.1.call-done = f32[1024,2048]{0,1:T(8,128)} async-done(((f32[1024,128]{0,1:T(8,128)}), f32[1024,2048]{0,1:T(8,128)}) %all-gather.11.cloned.1.call-update) | async-done | bytes 8388624 | tf_op jit(solution)/shard_map/all_gather | solution.py:60
  266.1 17.0 %fusion.5 = f32[1024,256]{1,0:T(8,128)} fusion(f32[1024,2048]{0,1:T(8,128)} %all-gather.11.cloned.1.call-done, f32[2048,256]{1,0:T(8,128)} %all-gather.13.cloned.1.call-done), kind=kOutput, calls=%fused_computation.22 | convolution fusion | flops 6442450944 | bytes 11534336 | tf_op jit(solution)/shard_map/dot_general | solution.py:39
  283.2 1.7 mul.109
  284.9 2.5 mul.110
  288.0 20.8 %all-reduce.6.cloned.1.call-done = f32[1024,256]{1,0:T(8,128)} async-done(((f32[1024,256]{1,0:T(8,128)}), f32[1024,256]{1,0:T(8,128)}) %all-reduce.6.cloned.1.call-update) | async-done | bytes 1048592 | tf_op jit(solution)/shard_map/psum | solution.py:62
  308.8 1.4 multiply_add_fusion
  310.2 0.9 dynamic-slice_multiply_fusion
  311.2 0.3 copy.12
  311.5 0.8 dynamic-slice_multiply_fusion.1
  312.4 0.3 all-reduce.8.cloned.1.call-start
  312.6 29.0 %all-gather.17.cloned.1.call-done = f32[2048,256]{1,0:T(8,128)} async-done(((f32[512,256]{1,0:T(8,128)}), f32[2048,256]{1,0:T(8,128)}) %all-gather.17.cloned.1.call-update) | async-done | bytes 2097168 | tf_op jit(solution)/shard_map/all_gather | solution.py:58
  341.7 74.7 %all-gather.15.cloned.1.call-done = f32[1024,2048]{0,1:T(8,128)} async-done(((f32[1024,128]{0,1:T(8,128)}), f32[1024,2048]{0,1:T(8,128)}) %all-gather.15.cloned.1.call-update) | async-done | bytes 8388624 | tf_op jit(solution)/shard_map/all_gather | solution.py:60
  416.3 17.0 %fusion.6 = f32[1024,256]{1,0:T(8,128)} fusion(f32[1024,2048]{0,1:T(8,128)} %all-gather.15.cloned.1.call-done, f32[2048,256]{1,0:T(8,128)} %all-gather.17.cloned.1.call-done), kind=kOutput, calls=%fused_computation.23 | convolution fusion | flops 6442450944 | bytes 11534336 | tf_op jit(solution)/shard_map/dot_general | solution.py:39
  434.0 25.0 %all-reduce.8.cloned.1.call-done = f32[1024,256]{1,0:T(8,128)} async-done(((f32[1024,256]{1,0:T(8,128)}), f32[1024,256]{1,0:T(8,128)}) %all-reduce.8.cloned.1.call-update) | async-done | bytes 1048592 | tf_op jit(solution)/shard_map/psum | solution.py:62
  459.0 2.1 fusion
  461.1 2.1 pad_maximum_fusion
  463.1 64.1 %psum.31 = f32[3]{0:T(128)} all-reduce(f32[3]{0:T(128)S(1)} %pad_maximum_fusion), channel_id=1, replica_groups=mesh['row'=4,'col'=16,'depth'=2] {'row','col','depth'}, use_global_device_ids=true, to_apply=%region_6.7 | all-reduce | flops 3 | bytes 24 | tf_op jit(solution)/shard_map/psum | solution.py:68
  527.2 2.4 add_multiply_fusion
  (34 shorter events, 0.9 us)
Async XLA Ops:
  7.2 2.1 copy-start
  7.2 34.1 %all-gather.9.cloned.1.call-start = ((), (), s32[]{:S(2)}) async-start(), calls=%async_computation.1 | async-start | bytes 2621440 | tf_op jit(solution)/shard_map/all_gather | solution.py:58
  9.2 106.7 %all-gather.7.cloned.1.call-start = ((), (), s32[]{:S(2)}) async-start(), calls=%async_computation | async-start | bytes 8912896 | tf_op jit(solution)/shard_map/all_gather | solution.py:60
  10.5 122.5 %copy-start.2 = (s32[3]{0:T(128)S(1)}, s32[3]{0:T(128)}, u32[]{:S(2)}) copy-start(s32[3]{0:T(128)} %param.5) | copy-start | bytes 40
  10.5 123.8 %copy-start.3 = (s32[16,4]{0,1:T(4,128)S(1)}, s32[16,4]{0,1:T(4,128)}, u32[]{:S(2)}) copy-start(s32[16,4]{0,1:T(4,128)} %param.4) | copy-start | bytes 772
  10.5 148.1 %all-reduce.4.cloned.1.call-start = ((), (), s32[]{:S(2)}) async-start(), calls=%async_computation.2 | async-start | bytes 2097152 | tf_op jit(solution)/shard_map/psum | solution.py:62
  132.9 58.4 %all-gather.13.cloned.1.call-start = ((), (), s32[]{:S(2)}) async-start(), calls=%async_computation.4 | async-start | bytes 2621440 | tf_op jit(solution)/shard_map/all_gather | solution.py:58
  160.8 105.3 %all-gather.11.cloned.1.call-start = ((), (), s32[]{:S(2)}) async-start(), calls=%async_computation.3 | async-start | bytes 8912896 | tf_op jit(solution)/shard_map/all_gather | solution.py:60
  162.3 146.5 %all-reduce.6.cloned.1.call-start = ((), (), s32[]{:S(2)}) async-start(), calls=%async_computation.5 | async-start | bytes 2097152 | tf_op jit(solution)/shard_map/psum | solution.py:62
  283.1 58.5 %all-gather.17.cloned.1.call-start = ((), (), s32[]{:S(2)}) async-start(), calls=%async_computation.7 | async-start | bytes 2621440 | tf_op jit(solution)/shard_map/all_gather | solution.py:58
  311.1 105.2 %all-gather.15.cloned.1.call-start = ((), (), s32[]{:S(2)}) async-start(), calls=%async_computation.6 | async-start | bytes 8912896 | tf_op jit(solution)/shard_map/all_gather | solution.py:60
  312.4 146.6 %copy-start.1 = (f32[1024,256]{1,0:T(8,128)S(1)}, f32[1024,256]{1,0:T(8,128)}, u32[]{:S(2)}) copy-start(f32[1024,256]{1,0:T(8,128)} %all-reduce.6.cloned.1.call-done) | copy-start | bytes 3145732
  312.4 146.6 %all-reduce.8.cloned.1.call-start = ((), (), s32[]{:S(2)}) async-start(), calls=%async_computation.8 | async-start | bytes 2097152 | tf_op jit(solution)/shard_map/psum | solution.py:62
Sparse Core Ops, SparseCore 0:
  9.7 31.5 all-gather.8
  44.0 71.9 all-gather.6
  133.1 25.4 all-reduce.3
  160.9 30.3 all-gather.12
  194.2 71.9 all-gather.10
  283.3 25.4 all-reduce.5
  311.2 30.3 all-gather.16
  344.4 71.9 all-gather.14
  433.5 25.4 all-reduce.7
where the time goes:
time: 540 us; the launch traced here: 536 us
  waiting for transfers between devices  383 us (71%)
  blocking collectives  64.1 us (12%)
  matrix products  51 us (9%)
  between operations  15.9 us (3%)
  other arithmetic  12.8 us (2%)
  local copies, waits for them, and re-layouts  9.01 us (2%)
    all_gather x3, waiting for transfers between devices, per_device(): lax.all_gather(left_piece, 'col', axis=1, tiled=True)  224 us
    all_gather x3, waiting for transfers between devices, per_device(): column_panel = lax.all_gather(right_piece, 'row', axis=0, tiled=True)  88.6 us
    psum x3, waiting for transfers between devices, per_device(): square = lax.psum(partial_value, 'depth')  69.8 us
    psum x1, blocking collectives, per_device(): traces = lax.psum(stacked, ('row', 'col', 'depth'))  64.1 us
    dot_general x3, matrix products, full_product(): jnp.dot(left_part, right_part, precision=lax.Precision.HIGHEST, preferred...  51 us
  transfers between devices with their start and end apart: 9, of which 9 were waited for; matrix products, arithmetic and copies ran while one was open for 2% of the time, Pallas kernels for 0%

commit v1 on v0

v1 whole, which is shorter than its diff:
```python
import functools

import jax
import jax.numpy as jnp
from jax import lax
from jax.experimental import pallas as pl
from jax.experimental.pallas import tpu as pltpu
from jax.sharding import PartitionSpec as P

MESH = pl.DeviceIdType.MESH
STEPS = 3
BS = 64
BLK = 1024
SLAB = 128
CH = 32
ROLES = (("x", "z", "y"), ("z", "y", "x"), ("y", "x", "z"))
PLUS_ORDER = (0, 1, 2, 3)
MINUS_ORDER = (2, 3, 0, 1)
F32 = jnp.float32
BF16 = jnp.bfloat16


def nt_dot(left, right):
    return lax.dot_general(left, right, (((1,), (1,)), ((), ())), preferred_element_type=F32)


def split(value):
    high = value.astype(BF16)
    return high, (value - high.astype(F32)).astype(BF16)


def body(
    dens, pat, br, out, tr_out,
    pbuf, qbuf, phi, plo, qhi, qlo, obuf, r1, r2, patf, gbuf, vsend, vcore, vaxis, fin,
    ag_s, ag_r, cx_s, cx_r, bc_s, bc_r, rs_s, rs_r, pt_s, pt_r, tr_s, tr_r, fx_s, fx_r,
):
    col = lax.axis_index("col")
    k = lax.axis_index("depth")
    pos = {"x": lax.axis_index("row"), "y": lax.rem(col, 4), "z": lax.div(col, 4)}
    other = 1 - k

    def wrap(value):
        return lax.rem(value + 8, 4)

    def device(x, y, z, core):
        return (x, z * 4 + y, core)

    def at(axis, delta):
        place = dict(pos)
        place[axis] = wrap(place[axis] + delta)
        return device(place["x"], place["y"], place["z"], k)

    partner = device(pos["x"], pos["y"], pos["z"], other)

    def rcopy(src, dst, send, recv, dev):
        return pltpu.make_async_remote_copy(
            src_ref=src, dst_ref=dst, send_sem=send, recv_sem=recv, device_id=dev, device_id_type=MESH
        )

    own0 = pos["y"] * 2 + k
    for i in range(8):
        piece = dens[i * 128:(i + 1) * 128, pl.ds(pl.multiple_of(k * 128, 128), 128)]
        pbuf[0, own0, :, i * 128:(i + 1) * 128] = piece.T
    patf[...] = jnp.zeros_like(patf)
    vsend[0] = jnp.zeros((8, 128), F32)
    patf[:, 0:4] = pat[...].astype(F32)

    barrier = pltpu.get_barrier_semaphore()
    greet = [partner]
    for axis in ("x", "y", "z"):
        for delta in (1, -1, 2):
            greet.append(at(axis, delta))
    for i in range(4):
        greet.append(device(pos["y"], i, pos["z"], other))
        greet.append(device(pos["x"], i, pos["y"], other))
    for dev in greet:
        pl.semaphore_signal(barrier, inc=1, device_id=dev, device_id_type=MESH)
    pl.semaphore_wait(barrier, len(greet))

    def pattern_copies():
        found = []
        for i in range(4):
            found.append(rcopy(patf, gbuf.at[0, pos["y"]], pt_s.at[0, i], pt_r.at[0, pos["y"]],
                               device(i, pos["x"], pos["z"], other)))
            found.append(rcopy(patf, gbuf.at[1, pos["y"]], pt_s.at[1, i], pt_r.at[1, pos["y"]],
                               device(pos["x"], pos["z"], i, other)))
        return found

    def pattern_wait(s):
        for i in range(4):
            rcopy(patf, gbuf.at[s, i], pt_s.at[s, i], pt_r.at[s, i], partner).wait_recv()

    def square_sum(s, slab):
        total = jnp.zeros((1, BLK), F32)
        for i in range(4):
            part = pbuf[s, slab, i * 32:(i + 1) * 32, :]
            total = total + jnp.sum(part * part, axis=0, keepdims=True)
        vsend[0, s:s + 1, :] = jnp.broadcast_to(jnp.sum(total, axis=1, keepdims=True), (1, 128))

    def trace_core_start():
        rcopy(vsend.at[0], vcore, tr_s.at[0, 0], tr_r.at[0, 0], partner).start()

    def trace_core_end():
        copy = rcopy(vsend.at[0], vcore, tr_s.at[0, 0], tr_r.at[0, 0], partner)
        copy.wait_recv()
        copy.wait_send()
        vsend[1] = vsend[0] + vcore[...]

    def trace_axis_copies(stage, axis):
        me = pos[axis]
        return [
            rcopy(vsend.at[stage], vaxis.at[stage, me], tr_s.at[stage, d], tr_r.at[stage, me], at(axis, d))
            for d in (1, 2, 3)
        ]

    def trace_axis_start(stage, axis):
        for copy in trace_axis_copies(stage, axis):
            copy.start()
        vaxis[stage, pos[axis]] = vsend[stage]

    def trace_axis_end(stage, axis):
        for d in (1, 2, 3):
            src = wrap(pos[axis] + d)
            rcopy(vsend.at[stage], vaxis.at[stage, src], tr_s.at[stage, d], tr_r.at[stage, src], partner).wait_recv()
        for copy in trace_axis_copies(stage, axis):
            copy.wait_send()
        vsend[stage + 1] = (vaxis[stage, 0] + vaxis[stage, 1]) + (vaxis[stage, 2] + vaxis[stage, 3])

    for s in range(STEPS):
        an, bn, cn = ROLES[s]
        a, b, c = pos[an], pos[bn], pos[cn]
        d = wrap(b - c)
        root = d == 0
        own = c * 2 + k

        def rows(j):
            return pl.ds(j * CH, CH)

        def ag_copy(direction, i):
            sign = 1 if direction == 0 else -1
            order = PLUS_ORDER if direction == 0 else MINUS_ORDER
            if i < 4:
                slab, chunk = own, order[i]
            else:
                slab, chunk = wrap(c - sign) * 2 + k, order[i - 4]
            ref = pbuf.at[s, slab, rows(chunk)]
            return rcopy(ref, ref, ag_s.at[s, direction, i], ag_r.at[s, direction, i], at(cn, sign))

        def ag_arrival(direction, i):
            sign = 1 if direction == 0 else -1
            order = PLUS_ORDER if direction == 0 else MINUS_ORDER
            if i < 4:
                return wrap(c - sign), order[i]
            return wrap(c + 2), order[i - 4]

        def ag_wait(direction, i):
            q, chunk = ag_arrival(direction, i)
            ref = pbuf.at[s, q * 2 + k, rows(chunk)]
            rcopy(ref, ref, ag_s.at[s, direction, i], ag_r.at[s, direction, i], partner).wait_recv()

        def cx_copy(i):
            if i == 0:
                ref = pbuf.at[s, own]
            else:
                q, chunk = ag_arrival((i - 1) % 2, (i - 1) // 2)
                ref = pbuf.at[s, q * 2 + k, rows(chunk)]
            return rcopy(ref, ref, cx_s.at[s, i], cx_r.at[s, i], partner)

        def cx_wait(i):
            if i == 0:
                ref = pbuf.at[s, c * 2 + other]
            else:
                q, chunk = ag_arrival((i - 1) % 2, (i - 1) // 2)
                ref = pbuf.at[s, q * 2 + other, rows(chunk)]
            rcopy(ref, ref, cx_s.at[s, i], cx_r.at[s, i], partner).wait_recv()

        def bc_place(direction, seq):
            half = lax.div(seq, 2)
            near = -1 if direction == 0 else 1
            offset = jnp.where(half == 0, 0, jnp.where(half == 1, near, jnp.where(half == 2, -near, 2)))
            chunk = lax.rem(seq, 2) + (0 if direction == 0 else 2)
            return wrap(c + offset), pl.multiple_of(chunk * CH, CH)

        def bc_copy(direction, seq, from_root):
            q, row = bc_place(direction, seq)
            dst = qbuf.at[s, q, pl.ds(row, CH)]
            src = pbuf.at[s, q * 2 + k, pl.ds(row, CH)] if from_root else dst
            return rcopy(src, dst, bc_s.at[s, direction, seq], bc_r.at[s, direction, seq],
                         at(bn, 1 if direction == 0 else -1))

        for i in range(4):
            ag_copy(0, i).start()
            ag_copy(1, i).start()
        cx_copy(0).start()

        @pl.when(root)
        def _():
            for seq in range(2):
                bc_copy(0, jnp.int32(seq), True).start()
                bc_copy(1, jnp.int32(seq), True).start()

        if s == 0:
            for copy in pattern_copies():
                copy.start()
        square_sum(s, own)
        if s == 2:
            trace_core_start()

        for tick in range(10):
            if tick < 6:
                for direction in (0, 1):
                    ag_wait(direction, tick)
                    if tick < 2:
                        ag_copy(direction, tick + 4).start()
                for direction in (0, 1):
                    cx_copy(1 + 2 * tick + direction).start()

                @pl.when(root)
                def _():
                    bc_copy(0, jnp.int32(tick + 2), True).start()
                    bc_copy(1, jnp.int32(tick + 2), True).start()

            for direction in (0, 1):
                lag = d - 1 if direction == 0 else 3 - d
                seq = tick - lag

                @pl.when(jnp.logical_and(d > 0, jnp.logical_and(seq >= 0, seq < 8)))
                def _():
                    copy = bc_copy(direction, seq, False)
                    copy.wait_recv()

                    @pl.when(lag < 2)
                    def _():
                        copy.start()

        for i in range(13):
            cx_wait(i)
        if s == 2:
            trace_core_end()
            trace_axis_start(1, "x")

        @pl.loop(0, 8)
        def _(j):
            row = pl.multiple_of(j * SLAB, SLAB)
            high, low = split(pbuf[s, j])
            phi[pl.ds(row, SLAB), :] = high
            plo[pl.ds(row, SLAB), :] = low

        @pl.when(root)
        def _():
            @pl.loop(0, 4)
            def _(q):
                row = pl.multiple_of(q * SLAB, SLAB)
                high, low = split(pbuf[s, q * 2 + k])
                qhi[pl.ds(row, SLAB), :] = high
                qlo[pl.ds(row, SLAB), :] = low

        @pl.when(jnp.logical_not(root))
        def _():
            @pl.loop(0, 4)
            def _(q):
                row = pl.multiple_of(q * SLAB, SLAB)
                high, low = split(qbuf[s, q])
                qhi[pl.ds(row, SLAB), :] = high
                qlo[pl.ds(row, SLAB), :] = low

        weight = br[s].astype(F32)
        scale = 1.0 - 2.0 * weight
        linear = 2.0 * weight * (a == b).astype(F32)

        @pl.loop(0, 4)
        def _(n):
            at_col = pl.multiple_of(n * 256, 256)
            high = phi[pl.ds(at_col, 256), :]
            low = plo[pl.ds(at_col, 256), :]
            value = nt_dot(qhi[...], high) + nt_dot(qhi[...], low) + nt_dot(qlo[...], high)
            same = qhi[:, pl.ds(at_col, 256)].astype(F32) + qlo[:, pl.ds(at_col, 256)].astype(F32)
            obuf[:, pl.ds(at_col, 256)] = scale * value + linear * same

        def slab_rows(q, first, count):
            return pl.ds(pl.multiple_of(q * SLAB + first, 64), count)

        up, down, far = wrap(a + 1), wrap(a - 1), wrap(a + 2)

        def rs_copy(direction, i):
            sign = 1 if direction == 0 else -1
            near = up if direction == 0 else down
            first = 0 if direction == 0 else 64
            if i == 0:
                src, dst = obuf.at[slab_rows(far, first, 64)], r1.at[s, direction]
            elif i == 1:
                src, dst = obuf.at[slab_rows(near, 64 - first, 64)], r2.at[s, direction, pl.ds(64 - first, 64)]
            else:
                src, dst = obuf.at[slab_rows(near, first, 64)], r2.at[s, direction, pl.ds(first, 64)]
            return rcopy(src, dst, rs_s.at[s, direction, i], rs_r.at[s, direction, i], at(an, sign))

        for i in (0, 1):
            for direction in (0, 1):
                rs_copy(direction, i).start()
        if s == 2:
            trace_axis_end(1, "x")
            trace_axis_start(2, "y")
        for direction in (0, 1):
            rs_copy(direction, 0).wait_recv()
            near = up if direction == 0 else down
            part = slab_rows(near, 0 if direction == 0 else 64, 64)
            obuf[part, :] = obuf[part, :] + r1[s, direction]
            rs_copy(direction, 2).start()
        if s == 2:
            trace_axis_end(2, "y")
            trace_axis_start(3, "z")

        if s < 2:
            pattern_wait(s)
            line = lax.broadcasted_iota(jnp.int32, (SLAB, 16), 0)
            block = lax.broadcasted_iota(jnp.int32, (SLAB, 16), 1)
            pick = (block == a * 4 + k * 2 + line // BS).astype(F32)
            left = lax.broadcasted_iota(jnp.int32, (128, 256), 0)
            right = lax.broadcasted_iota(jnp.int32, (128, 256), 1)
            spread = (left == right // BS).astype(F32)
        for i in (1, 2):
            for direction in (0, 1):
                rs_copy(direction, i).wait_recv()
        for i in range(4):
            lanes = slice(i * 256, (i + 1) * 256)
            value = obuf[slab_rows(a, 0, SLAB), lanes] + r2[s, 0, :, lanes] + r2[s, 1, :, lanes]
            if s < 2:
                chosen = jnp.dot(pick, gbuf[s, i], preferred_element_type=F32)
                pbuf[s + 1, a * 2 + k, :, lanes] = value * jnp.dot(chosen, spread, preferred_element_type=F32)
            else:
                fin[k, :, lanes] = value

        for direction in (0, 1):
            for i in range(6):
                ag_copy(direction, i).wait_send()
            for i in range(3):
                rs_copy(direction, i).wait_send()

            @pl.when(d != (3 if direction == 0 else 1))
            def _():
                for seq in range(8):
                    bc_copy(direction, jnp.int32(seq), False).wait_send()
        for i in range(13):
            cx_copy(i).wait_send()
        if s == 0:
            for copy in pattern_copies():
                copy.wait_send()

    last = rcopy(fin.at[k], fin.at[k], fx_s, fx_r, partner)
    last.start()
    trace_axis_end(3, "z")
    tr_out[...] = vsend[4]
    left = lax.broadcasted_iota(jnp.int32, (128, 256), 0)
    right = lax.broadcasted_iota(jnp.int32, (128, 256), 1)
    spread = (left == right // BS).astype(F32)
    line = lax.broadcasted_iota(jnp.int32, (128, 16), 0)
    block = lax.broadcasted_iota(jnp.int32, (128, 16), 1)
    rcopy(fin.at[other], fin.at[other], fx_s, fx_r, partner).wait_recv()
    for i in range(8):
        pick = (block == i * 2 + line // BS).astype(F32)
        chosen = jnp.dot(pick, patf[...], preferred_element_type=F32)
        mask = jnp.dot(chosen, spread, preferred_element_type=F32)
        for half in range(2):
            lanes = slice(half * 128, (half + 1) * 128)
            part = fin[half, :, i * 128:(i + 1) * 128].T
            out[i * 128:(i + 1) * 128, lanes] = part * mask[:, lanes]
    last.wait_send()


def per_device(density, pattern, branches):
    vmem = pl.BlockSpec(memory_space=pltpu.VMEM)
    dma = pltpu.SemaphoreType.DMA
    purified, traces = pl.pallas_call(
        body,
        out_shape=(
            jax.ShapeDtypeStruct((BLK, 256), F32),
            jax.ShapeDtypeStruct((8, 128), F32),
        ),
        in_specs=[vmem, vmem, pl.BlockSpec(memory_space=pltpu.SMEM)],
        out_specs=(vmem, vmem),
        scratch_shapes=[
            pltpu.VMEM((STEPS, 8, SLAB, BLK), F32),
            pltpu.VMEM((STEPS, 4, SLAB, BLK), F32),
            pltpu.VMEM((BLK, BLK), BF16),
            pltpu.VMEM((BLK, BLK), BF16),
            pltpu.VMEM((512, BLK), BF16),
            pltpu.VMEM((512, BLK), BF16),
            pltpu.VMEM((512, BLK), F32),
            pltpu.VMEM((STEPS, 2, 64, BLK), F32),
            pltpu.VMEM((STEPS, 2, SLAB, BLK), F32),
            pltpu.VMEM((16, 128), F32),
            pltpu.VMEM((2, 4, 16, 128), F32),
            pltpu.VMEM((5, 8, 128), F32),
            pltpu.VMEM((8, 128), F32),
            pltpu.VMEM((4, 4, 8, 128), F32),
            pltpu.VMEM((2, SLAB, BLK), F32),
            dma((STEPS, 2, 6)), dma((STEPS, 2, 6)),
            dma((STEPS, 13)), dma((STEPS, 13)),
            dma((STEPS, 2, 8)), dma((STEPS, 2, 8)),
            dma((STEPS, 2, 3)), dma((STEPS, 2, 3)),
            dma((2, 4)), dma((2, 4)),
            dma((4, 4)), dma((4, 4)),
            dma, dma,
        ],
        compiler_params=pltpu.CompilerParams(
            collective_id=0, has_side_effects=True, vmem_limit_bytes=56 * 2**20
        ),
        name="purify",
    )(density, pattern, branches)
    return purified, traces[:STEPS, 0]


def solution(mesh):
    return jax.shard_map(
        per_device,
        mesh=mesh,
        in_specs=(P("row", "col"), P("row", "col"), P()),
        out_specs=(P("row", "col"), P()),
        check_vma=False,
    )
```

time: 540 us -> 205 us (0.38)
  waiting for transfers between devices: 383 us -> 0 us
  Pallas kernels: 0 us -> 199 us
  blocking collectives: 64.1 us -> 0 us
  matrix products: 51 us -> 0 us
  between operations: 15.9 us -> 0.64 us
  other arithmetic: 12.8 us -> 0 us
    all_gather x6 -> x0, waiting for transfers between devices: 313 us -> none  [the longest x3 224 us: per_device(): lax.all_gather(left_piece, 'col', axis=1, tiled=True)]
    pallas_call x0 -> x1, Pallas kernels: none -> 199 us  [per_device(): pl.pallas_call(body, out_shape=(jax.ShapeDtypeStruct((BLK, 256), F32), ja...]
    psum x3 -> x0, waiting for transfers between devices: 69.8 us -> none  [per_device(): square = lax.psum(partial_value, 'depth')]
    psum x1 -> x0, blocking collectives: 64.1 us -> none  [per_device(): traces = lax.psum(stacked, ('row', 'col', 'depth'))]
    dot_general x3 -> x0, matrix products: 51 us -> none  [full_product(): jnp.dot(left_part, right_part, precision=lax.Precision.HIGHEST, preferred...]
    mul x5 -> x0, other arithmetic: 5.82 us -> none  [apply_pattern(): shaped * kept_blocks.astype(jnp.float32)[:, None, :, None]]
  transfers between devices with their start and end apart: 9 -> 0, of which waited for: 9 -> 0; matrix products, arithmetic and copies ran while one was open for 2% -> 0% of each run, Pallas kernels for 0% -> 0%
where the time goes in v1:
time: 205 us
  Pallas kernels  199 us (97%)
  local copies, waits for them, and re-layouts  4.92 us (2%)
    pallas_call x1, Pallas kernels, per_device(): pl.pallas_call(body, out_shape=(jax.ShapeDtypeStruct((BLK, 256), F32), ja...  199 us

profile of v1, /device:TPU:37, one launch (start us, length us, event | category | flops | bytes accessed | tf_op | source)
XLA Modules:
  0.0 205.0 jit_solution(4975855916333792851)
XLA Ops:
  0.6 1.4 copy.6.pat
  2.0 199.4 %purify.1 = (f32[1024,256]{1,0:T(8,128)}, f32[8,128]{1,0:T(8,128)}) custom-call(f32[1024,256]{1,0:T(8,128)} %dens.1, s32[16,4]{1,0:T(8,128)} %copy.6.pat, s32[3]{0:T(128)} %br.1), custom_call_target="tpu_custom_call" | custom-call | tf_op jit(solution)/shard_map/purify/pallas_call | solution.py:373
  201.4 1.3 slice_reduce_fusion
  202.7 2.3 %copy.8 = f32[1024,256]{1,0:T(8,128)} copy(f32[1024,256]{1,0:T(8,128)} %get-tuple-element.8) | data formatting | bytes 2097152

commit v2 on v0

v2 whole, which is shorter than its diff:
```python
import functools

import jax
import jax.numpy as jnp
from jax import lax
from jax.experimental import pallas as pl
from jax.experimental.pallas import tpu as pltpu
from jax.sharding import PartitionSpec as P

MESH = pl.DeviceIdType.MESH
STEPS = 3
BS = 64
BLK = 1024
SLAB = 128
CH = 32
HALF = 16
LAG = 3
OFFSETS = (0, -1, 1, 2)
START_AT = (0.0, 34.0, 72.0)
ARRIVE = (
    {
        "direct": (4.5, 7.4, 11.8, 16.2), "handed": (9.0, 13.3, 17.7, 19.2), "split_p": (11.0, 15.3, 19.7, 21.2),
        "sum": 1.0, "tick": lambda t: 3.0 + 4.5 * (t > 0) + 1.5 * t + 1.5 * (t > 2),
        "piece": (19.8, 25.0, 30.0, 36.0), "product": (21.3, 25.3, 31.0, 37.0),
        "add_on": (26.0, 29.8, 34.5, 39.7), "finish": (31.0, 35.0, 39.8, 43.0),
    },
    {
        "direct": (6.0, 9.6, 14.0, 19.0), "handed": (9.5, 14.1, 19.1, 24.0), "split_p": (11.5, 16.1, 21.1, 26.0),
        "sum": 12.5, "tick": lambda t: 3.5 + 4.0 * (t > 0) + 1.5 * t + 1.5 * (t > 2),
        "piece": (22.0, 28.0, 30.0, 36.0), "product": (26.1, 28.1, 31.5, 37.0),
        "add_on": (31.0, 34.0, 36.5, 41.0), "finish": (36.0, 39.0, 42.0, 46.0),
    },
)
ROLES = (("x", "z", "y"), ("z", "y", "x"), ("y", "x", "z"))
F32 = jnp.float32
BF16 = jnp.bfloat16


def nt_dot(left, right):
    return lax.dot_general(left, right, (((1,), (1,)), ((), ())), preferred_element_type=F32)


def split(value):
    high = value.astype(BF16)
    return high, (value - high.astype(F32)).astype(BF16)


def lane_rows(i):
    unit = i // 2
    return [(2 * (i % 2) + q) * 256 + core * SLAB + unit * CH for q in (0, 1) for core in (0, 1)]


def body(
    dens, pat, br, out, tr_out,
    pbuf, qbuf, phi, plo, qcat, obuf, r1, r2, patf, gbuf, mbuf, vsend, vcore, vaxis, fin,
    ag_s, ag_r, af_s, af_r, cx_s, cx_r, bc_s, bc_r, rs_s, rs_r, pt_s, pt_r, tr_s, tr_r, fx_s, fx_r,
):
    col = lax.axis_index("col")
    k = lax.axis_index("depth")
    pos = {"x": lax.axis_index("row"), "y": lax.rem(col, 4), "z": lax.div(col, 4)}
    other = 1 - k

    def wrap(value):
        return lax.rem(value + 8, 4)

    def device(x, y, z, core):
        return (x, z * 4 + y, core)

    def at(axis, delta):
        place = dict(pos)
        place[axis] = wrap(place[axis] + delta)
        return device(place["x"], place["y"], place["z"], k)

    partner = device(pos["x"], pos["y"], pos["z"], other)

    def rcopy(src, dst, send, recv, dev):
        return pltpu.make_async_remote_copy(
            src_ref=src, dst_ref=dst, send_sem=send, recv_sem=recv, device_id=dev, device_id_type=MESH
        )

    barrier = pltpu.get_barrier_semaphore()
    greet = [partner]
    for axis in ("x", "y", "z"):
        for delta in (1, -1, 2):
            greet.append(at(axis, delta))
    for i in range(4):
        greet.append(device(pos["y"], i, pos["z"], other))
        greet.append(device(pos["x"], i, pos["y"], other))
    for dev in greet:
        pl.semaphore_signal(barrier, inc=1, device_id=dev, device_id_type=MESH)

    for i in range(8):
        mine = pl.ds(pl.multiple_of(k * 128, 128), 128)
        piece = jnp.concatenate([dens[row:row + CH, mine] for row in lane_rows(i)], axis=0)
        pbuf[0, pos["y"], k, :, i * 128:(i + 1) * 128] = piece.T
    patf[...] = jnp.zeros_like(patf)
    vsend[0] = jnp.zeros((8, 128), F32)
    patf[:, 0:4] = pat[...].astype(F32)
    pl.semaphore_wait(barrier, len(greet))

    def pattern_copies():
        found = []
        for i in range(4):
            found.append(rcopy(patf, gbuf.at[0, pos["y"]], pt_s.at[0, i], pt_r.at[0, pos["y"]],
                               device(i, pos["x"], pos["z"], other)))
            found.append(rcopy(patf, gbuf.at[1, pos["y"]], pt_s.at[1, i], pt_r.at[1, pos["y"]],
                               device(pos["x"], pos["z"], i, other)))
        return found

    def pattern_wait(s):
        for i in range(4):
            rcopy(patf, gbuf.at[s, i], pt_s.at[s, i], pt_r.at[s, i], partner).wait_recv()

    def square_sum(s, slab):
        total = jnp.zeros((1, BLK), F32)
        for i in range(4):
            part = pbuf[s, slab, k, i * CH:(i + 1) * CH, :]
            total = total + jnp.sum(part * part, axis=0, keepdims=True)
        vsend[0, s:s + 1, :] = jnp.broadcast_to(jnp.sum(total, axis=1, keepdims=True), (1, 128))

    def trace_core():
        return rcopy(vsend.at[0], vcore, tr_s.at[0, 0], tr_r.at[0, 0], partner)

    def trace_core_end():
        trace_core().wait()
        vsend[1] = vsend[0] + vcore[...]

    def trace_axis_copies(stage, axis):
        me = pos[axis]
        return [
            rcopy(vsend.at[stage], vaxis.at[stage, me], tr_s.at[stage, d], tr_r.at[stage, me], at(axis, d))
            for d in (1, 2, 3)
        ]

    def trace_axis_start(stage, axis):
        for copy in trace_axis_copies(stage, axis):
            copy.start()
        vaxis[stage, pos[axis]] = vsend[stage]

    def trace_axis_end(stage, axis):
        for d in (1, 2, 3):
            src = wrap(pos[axis] + d)
            rcopy(vsend.at[stage], vaxis.at[stage, src], tr_s.at[stage, d], tr_r.at[stage, src], partner).wait_recv()
        for copy in trace_axis_copies(stage, axis):
            copy.wait_send()
        vsend[stage + 1] = (vaxis[stage, 0] + vaxis[stage, 1]) + (vaxis[stage, 2] + vaxis[stage, 3])

    def fin_copy(j, core):
        ref = fin.at[core, pl.ds(j * CH, CH)]
        return rcopy(ref, ref, fx_s.at[j], fx_r.at[j], partner)

    def make_step(s):
        step = {}
        an, bn, cn = ROLES[s]
        a, b, c = pos[an], pos[bn], pos[cn]
        d = wrap(b - c)
        root = d == 0
        up, down, far = wrap(a + 1), wrap(a - 1), wrap(a + 2)

        def rows(j):
            return pl.ds(j * CH, CH)

        def half_rows(j, direction):
            return pl.ds(j * CH + direction * HALF, HALF)

        def sign(direction):
            return 1 - 2 * direction

        def ag_copy(direction, j):
            ref = pbuf.at[s, c, k, rows(j)]
            return rcopy(ref, ref, ag_s.at[s, direction, j], ag_r.at[s, direction, j], at(cn, sign(direction)))

        def ag_wait(direction, j):
            ref = pbuf.at[s, wrap(c - sign(direction)), k, rows(j)]
            rcopy(ref, ref, ag_s.at[s, direction, j], ag_r.at[s, direction, j], partner).wait_recv()

        def af_copy(direction, j):
            ref = pbuf.at[s, wrap(c - sign(direction)), k, half_rows(j, direction)]
            return rcopy(ref, ref, af_s.at[s, direction, j], af_r.at[s, direction, j], at(cn, sign(direction)))

        def af_wait(direction, j):
            ref = pbuf.at[s, wrap(c + 2), k, half_rows(j, direction)]
            rcopy(ref, ref, af_s.at[s, direction, j], af_r.at[s, direction, j], partner).wait_recv()

        def cx_copy(j, i):
            ref = pbuf.at[s, wrap(c + OFFSETS[i]), k, rows(j)]
            return rcopy(ref, ref, cx_s.at[s, j, i], cx_r.at[s, j, i], partner)

        def cx_wait(j, i):
            ref = pbuf.at[s, wrap(c + OFFSETS[i]), other, rows(j)]
            rcopy(ref, ref, cx_s.at[s, j, i], cx_r.at[s, j, i], partner).wait_recv()

        def bc_copy(direction, seq, from_root):
            j = lax.div(seq, 4)
            part = lax.rem(seq, 4)
            q = wrap(c + jnp.where(part == 1, -1, jnp.where(part == 2, 1, jnp.where(part == 3, 2, 0))))
            place = pl.ds(pl.multiple_of(j * CH + direction * HALF, HALF), HALF)
            dst = qbuf.at[s, q, place]
            src = pbuf.at[s, q, k, place] if from_root else dst
            return rcopy(src, dst, bc_s.at[s, direction, seq], bc_r.at[s, direction, seq], at(bn, sign(direction)))

        def bc_root(*seqs):
            @pl.when(root)
            def _():
                for seq in seqs:
                    bc_copy(0, jnp.int32(seq), True).start()
                    bc_copy(1, jnp.int32(seq), True).start()

        def bc_tick(tick):
            for direction in (0, 1):
                hops = d - 1 if direction == 0 else 3 - d
                seq = tick - LAG * hops

                @pl.when(jnp.logical_and(d > 0, jnp.logical_and(seq >= 0, seq < 16)))
                def _():
                    copy = bc_copy(direction, seq, False)
                    copy.wait_recv()

                    @pl.when(hops < 2)
                    def _():
                        copy.start()

        def ready(j):
            ag_copy(0, j).start()
            ag_copy(1, j).start()
            bc_root(4 * j)
            cx_copy(j, 0).start()

        def direct(j):
            for direction in (0, 1):
                ag_wait(direction, j)
                af_copy(direction, j).start()
            if s == 0 and j < 2:
                ready(j + 2)
            cx_copy(j, 1).start()
            cx_copy(j, 2).start()
            bc_root(4 * j + 1, 4 * j + 2)

        def handed(j):
            for direction in (0, 1):
                af_wait(direction, j)
            cx_copy(j, 3).start()
            bc_root(4 * j + 3)

        def split_p(j):
            for i in range(4):
                cx_wait(j, i)

            @pl.loop(0, 8)
            def _(i):
                row = pl.multiple_of(j * 8 * CH + i * CH, CH)
                high, low = split(pbuf[s, lax.div(i, 2), lax.rem(i, 2), rows(j)])
                phi[s % 2, pl.ds(row, CH), :] = high
                plo[s % 2, pl.ds(row, CH), :] = low

        def split_q(j):
            def halves(read):
                for q in range(4):
                    high, low = split(read(q))
                    qcat[j, q * CH:(q + 1) * CH, :] = high
                    qcat[j, SLAB + q * CH:SLAB + (q + 1) * CH, :] = low

            @pl.when(root)
            def _():
                halves(lambda q: pbuf[s, q, k, rows(j)])

            @pl.when(jnp.logical_not(root))
            def _():
                halves(lambda q: qbuf[s, q, rows(j)])

        def product(j, first, last):
            weight = br[s].astype(F32)
            scale = 1.0 - 2.0 * weight
            linear = 2.0 * weight * (a == b).astype(F32)

            @pl.loop(first, last)
            def _(n):
                lanes = pl.ds(pl.multiple_of(n * 256, 256), 256)
                both = nt_dot(qcat[j], phi[s % 2, lanes, :])
                value = both[:SLAB] + both[SLAB:] + nt_dot(qcat[j, :SLAB, :], plo[s % 2, lanes, :])
                same = qcat[j, :SLAB, lanes].astype(F32) + qcat[j, SLAB:, lanes].astype(F32)
                obuf[s, j, :, lanes] = scale * value + linear * same

        def send_out(j):
            for i in (0, 1):
                for direction in (0, 1):
                    rs_copy(direction, i, j).start()

        def out_half(q, second):
            return pl.ds(pl.multiple_of(q * CH + second * HALF, HALF), HALF)

        def rs_copy(direction, i, j):
            near = up if direction == 0 else down
            if i == 0:
                src, dst = obuf.at[s, j, out_half(far, direction)], r1.at[s, direction, j]
            else:
                second = 1 - direction if i == 1 else direction
                src = obuf.at[s, j, out_half(near, second)]
                dst = r2.at[s, direction, j, pl.ds(second * HALF, HALF)]
            return rcopy(src, dst, rs_s.at[s, direction, j, i], rs_r.at[s, direction, j, i], at(an, sign(direction)))

        def add_on(j):
            for direction in (0, 1):
                rs_copy(direction, 0, j).wait_recv()
                place = out_half(up if direction == 0 else down, direction)
                obuf[s, j, place, :] = obuf[s, j, place, :] + r1[s, direction, j]
                rs_copy(direction, 2, j).start()

        def mask():
            pattern_wait(s)
            line = lax.broadcasted_iota(jnp.int32, (SLAB, 16), 0)
            block = lax.broadcasted_iota(jnp.int32, (SLAB, 16), 1)
            pick = (block == a * 4 + k * 2 + line // BS).astype(F32)
            left = lax.broadcasted_iota(jnp.int32, (128, 256), 0)
            right = lax.broadcasted_iota(jnp.int32, (128, 256), 1)
            chosen = [jnp.dot(pick, gbuf[s, q], preferred_element_type=F32) for q in range(4)]
            for pair in range(2):
                value = jnp.zeros((SLAB, 256), F32)
                for q in range(4):
                    wanted = (right % 64) // CH * 2 + pair
                    spread = jnp.logical_and(right // 64 == q, left == wanted).astype(F32)
                    value = value + jnp.dot(chosen[q], spread, preferred_element_type=F32)
                for i in (2 * pair, 2 * pair + 1):
                    mbuf[s, :, i * 256:(i + 1) * 256] = value

        def finish(j):
            for i in (1, 2):
                for direction in (0, 1):
                    rs_copy(direction, i, j).wait_recv()
            place = pl.ds(pl.multiple_of(a * CH, CH), CH)
            value = obuf[s, j, place, :] + (r2[s, 0, j] + r2[s, 1, j])
            if s < 2:
                pbuf[s + 1, a, k, rows(j), :] = value * mbuf[s, rows(j), :]
            else:
                fin[k, rows(j), :] = value
                fin_copy(j, k).start()

        def sent():
            for direction in (0, 1):
                for j in range(4):
                    ag_copy(direction, j).wait_send()
                    af_copy(direction, j).wait_send()

                @pl.when(d != (3 if direction == 0 else 1))
                def _():
                    for seq in range(16):
                        bc_copy(direction, jnp.int32(seq), False).wait_send()
            for j in range(4):
                for i in range(4):
                    cx_copy(j, i).wait_send()
            if s == 0:
                for copy in pattern_copies():
                    copy.wait_send()

        def rs_sent():
            for direction in (0, 1):
                for j in range(4):
                    for i in range(3):
                        rs_copy(direction, i, j).wait_send()

        step.update(locals())
        return step

    steps = [make_step(s) for s in range(STEPS)]
    steps[0]["ready"](0)
    steps[0]["ready"](1)
    for copy in pattern_copies():
        copy.start()

    events = {}

    def due(name, time, act, needs=()):
        time = max([time] + [events[need][0] for need in needs])
        events[name] = (time, len(events), act)

    def end_unit(s, j):
        steps[s]["finish"](j)
        if s + 1 < STEPS:
            steps[s + 1]["ready"](j)

    call = functools.partial
    for s in range(STEPS):
        now = steps[s]
        zero = START_AT[s]
        plan = ARRIVE[min(s, 1)]
        for j in range(4):
            begun = [("end", s - 1, j)] if s else []
            due(("direct", s, j), zero + plan["direct"][j], call(now["direct"], j), begun)
            due(("handed", s, j), zero + plan["handed"][j], call(now["handed"], j), [("direct", s, j)])
            due(("split_p", s, j), zero + plan["split_p"][j], call(now["split_p"], j), [("handed", s, j)])
        tick = plan["tick"]
        for t in range(16 + 2 * LAG):
            due(("tick", s, t), zero + tick(t), call(now["bc_tick"], t), [("tick", s, t - 1)] if t else begun)
        if s < 2:
            due(("mask", s), zero + 13.0, now["mask"], [("end", s - 1, 3)] if s else [])
        for j in range(4):
            due(("split_q", s, j), zero + plan["piece"][j], call(now["split_q"], j),
                [("tick", s, 4 * j + 3 + 2 * LAG), ("handed", s, j)])
            early = 3 if j == 0 else 0
            if early:
                due(("early", s, j), zero + plan["piece"][j], call(now["product"], j, 0, early),
                    [("split_q", s, j), ("split_p", s, early - 1)])
            due(("product", s, j), zero + plan["product"][j], call(now["product"], j, early, 4),
                [("split_q", s, j), ("split_p", s, 3)] + ([("early", s, j)] if early else []))
            due(("send_out", s, j), zero + plan["product"][j], call(now["send_out"], j), [("product", s, j)])
            due(("add_on", s, j), zero + plan["add_on"][j], call(now["add_on"], j), [("send_out", s, j)])
            due(("end", s, j), zero + plan["finish"][j], call(end_unit, s, j),
                [("add_on", s, j)] + ([("mask", s)] if s < 2 else []))
        due(("sum", s), zero + plan["sum"], call(square_sum, s, now["c"]), [("end", s - 1, 3)] if s else [])
        if s > 0:
            due(("sent", s - 1), zero + 16.0, steps[s - 1]["sent"], [("end", s - 1, 3)])
            due(("rs_sent", s - 1), zero + 20.0, steps[s - 1]["rs_sent"], [("end", s - 1, 3)])
        if s == 2:
            chain = [
                (0.0, lambda: trace_core().start()),
                (17.0, trace_core_end), (17.0, call(trace_axis_start, 1, "x")),
                (22.0, call(trace_axis_end, 1, "x")), (22.0, call(trace_axis_start, 2, "y")),
                (29.0, call(trace_axis_end, 2, "y")), (29.0, call(trace_axis_start, 3, "z")),
                (38.0, call(trace_axis_end, 3, "z")),
            ]
            before = ("sum", 2)
            for n, (time, act) in enumerate(chain):
                due(("trace", n), zero + time, act, [before])
                before = ("trace", n)
            due(("sent", s), zero + 39.0, now["sent"], [("tick", s, 15 + 2 * LAG), ("handed", s, 3)])
    for _, _, act in sorted(events.values(), key=lambda event: event[:2]):
        act()
    tr_out[...] = vsend[4]
    left = lax.broadcasted_iota(jnp.int32, (128, 256), 0)
    right = lax.broadcasted_iota(jnp.int32, (128, 256), 1)
    spread = (left == right // BS).astype(F32)
    line = lax.broadcasted_iota(jnp.int32, (128, 16), 0)
    block = lax.broadcasted_iota(jnp.int32, (128, 16), 1)
    steps[2]["rs_sent"]()
    for j in range(4):
        fin_copy(j, other).wait_recv()
    for i in range(8):
        here = [line // CH == n for n in range(4)]
        wanted = sum(jnp.where(here[n], row // BS, 0) for n, row in enumerate(lane_rows(i)))
        pick = (block == wanted).astype(F32)
        chosen = jnp.dot(pick, patf[...], preferred_element_type=F32)
        mask = jnp.dot(chosen, spread, preferred_element_type=F32)
        for half in range(2):
            lanes = slice(half * 128, (half + 1) * 128)
            part = fin[half, :, i * 128:(i + 1) * 128].T * mask[:, lanes]
            for n, row in enumerate(lane_rows(i)):
                out[row:row + CH, lanes] = part[n * CH:(n + 1) * CH]
    for j in range(4):
        fin_copy(j, k).wait_send()


def per_device(density, pattern, branches):
    vmem = pl.BlockSpec(memory_space=pltpu.VMEM)
    dma = pltpu.SemaphoreType.DMA
    purified, traces = pl.pallas_call(
        body,
        out_shape=(
            jax.ShapeDtypeStruct((BLK, 256), F32),
            jax.ShapeDtypeStruct((8, 128), F32),
        ),
        in_specs=[vmem, vmem, pl.BlockSpec(memory_space=pltpu.SMEM)],
        out_specs=(vmem, vmem),
        scratch_shapes=[
            pltpu.VMEM((STEPS, 4, 2, SLAB, BLK), F32),
            pltpu.VMEM((STEPS, 4, SLAB, BLK), F32),
            pltpu.VMEM((2, BLK, BLK), BF16),
            pltpu.VMEM((2, BLK, BLK), BF16),
            pltpu.VMEM((4, 2 * SLAB, BLK), BF16),
            pltpu.VMEM((STEPS, 4, SLAB, BLK), F32),
            pltpu.VMEM((STEPS, 2, 4, HALF, BLK), F32),
            pltpu.VMEM((STEPS, 2, 4, CH, BLK), F32),
            pltpu.VMEM((16, 128), F32),
            pltpu.VMEM((2, 4, 16, 128), F32),
            pltpu.VMEM((2, SLAB, BLK), F32),
            pltpu.VMEM((5, 8, 128), F32),
            pltpu.VMEM((8, 128), F32),
            pltpu.VMEM((4, 4, 8, 128), F32),
            pltpu.VMEM((2, SLAB, BLK), F32),
            dma((STEPS, 2, 4)), dma((STEPS, 2, 4)),
            dma((STEPS, 2, 4)), dma((STEPS, 2, 4)),
            dma((STEPS, 4, 4)), dma((STEPS, 4, 4)),
            dma((STEPS, 2, 16)), dma((STEPS, 2, 16)),
            dma((STEPS, 2, 4, 3)), dma((STEPS, 2, 4, 3)),
            dma((2, 4)), dma((2, 4)),
            dma((4, 4)), dma((4, 4)),
            dma((4,)), dma((4,)),
        ],
        compiler_params=pltpu.CompilerParams(
            collective_id=0, has_side_effects=True, vmem_limit_bytes=56 * 2**20
        ),
        name="purify",
    )(density, pattern, branches)
    return purified, traces[:STEPS, 0]


def solution(mesh):
    return jax.shard_map(
        per_device,
        mesh=mesh,
        in_specs=(P("row", "col"), P("row", "col"), P()),
        out_specs=(P("row", "col"), P()),
        check_vma=False,
    )
```

time: 540 us -> 171 us (0.32)
  waiting for transfers between devices: 383 us -> 0 us
  Pallas kernels: 0 us -> 164 us
  blocking collectives: 64.1 us -> 0 us
  matrix products: 51 us -> 0 us
  between operations: 15.9 us -> 0.64 us
  other arithmetic: 12.8 us -> 0 us
    all_gather x6 -> x0, waiting for transfers between devices: 313 us -> none  [the longest x3 224 us: per_device(): lax.all_gather(left_piece, 'col', axis=1, tiled=True)]
    pallas_call x0 -> x1, Pallas kernels: none -> 164 us  [per_device(): pl.pallas_call(body, out_shape=(jax.ShapeDtypeStruct((BLK, 256), F32), ja...]
    psum x3 -> x0, waiting for transfers between devices: 69.8 us -> none  [per_device(): square = lax.psum(partial_value, 'depth')]
    psum x1 -> x0, blocking collectives: 64.1 us -> none  [per_device(): traces = lax.psum(stacked, ('row', 'col', 'depth'))]
    dot_general x3 -> x0, matrix products: 51 us -> none  [full_product(): jnp.dot(left_part, right_part, precision=lax.Precision.HIGHEST, preferred...]
    mul x5 -> x0, other arithmetic: 5.82 us -> none  [apply_pattern(): shaped * kept_blocks.astype(jnp.float32)[:, None, :, None]]
  transfers between devices with their start and end apart: 9 -> 0, of which waited for: 9 -> 0; matrix products, arithmetic and copies ran while one was open for 2% -> 0% of each run, Pallas kernels for 0% -> 0%
where the time goes in v2:
time: 171 us; the launch traced here: 169 us
  Pallas kernels  164 us (96%)
  local copies, waits for them, and re-layouts  4.92 us (3%)
    pallas_call x1, Pallas kernels, per_device(): pl.pallas_call(body, out_shape=(jax.ShapeDtypeStruct((BLK, 256), F32), ja...  164 us
    unnamed x2, local copies, waits for them, and re-layouts  3.62 us

profile of v2, /device:TPU:37, one launch (start us, length us, event | category | flops | bytes accessed | tf_op | source)
XLA Modules:
  0.0 169.4 jit_solution(10858314592385723290)
XLA Ops:
  0.6 1.4 copy.6.pat
  2.0 163.9 %purify.1 = (f32[1024,256]{1,0:T(8,128)}, f32[8,128]{1,0:T(8,128)}) custom-call(f32[1024,256]{1,0:T(8,128)} %dens.1, s32[16,4]{1,0:T(8,128)} %copy.6.pat, s32[3]{0:T(128)} %br.1), custom_call_target="tpu_custom_call" | custom-call | tf_op jit(solution)/shard_map/purify/pallas_call | solution.py:455
  165.8 1.3 slice_reduce_fusion
  167.1 2.3 %copy.8 = f32[1024,256]{1,0:T(8,128)} copy(f32[1024,256]{1,0:T(8,128)} %get-tuple-element.8) | data formatting | bytes 2097152

commit v3 on v2

--- a/solution.py
+++ b/solution.py
@@ -14,23 +14,54 @@
 SLAB = 128
 CH = 32
 HALF = 16
-LAG = 3
 OFFSETS = (0, -1, 1, 2)
-START_AT = (0.0, 34.0, 72.0)
-ARRIVE = (
-    {
-        "direct": (4.5, 7.4, 11.8, 16.2), "handed": (9.0, 13.3, 17.7, 19.2), "split_p": (11.0, 15.3, 19.7, 21.2),
-        "sum": 1.0, "tick": lambda t: 3.0 + 4.5 * (t > 0) + 1.5 * t + 1.5 * (t > 2),
-        "piece": (19.8, 25.0, 30.0, 36.0), "product": (21.3, 25.3, 31.0, 37.0),
-        "add_on": (26.0, 29.8, 34.5, 39.7), "finish": (31.0, 35.0, 39.8, 43.0),
-    },
-    {
-        "direct": (6.0, 9.6, 14.0, 19.0), "handed": (9.5, 14.1, 19.1, 24.0), "split_p": (11.5, 16.1, 21.1, 26.0),
-        "sum": 12.5, "tick": lambda t: 3.5 + 4.0 * (t > 0) + 1.5 * t + 1.5 * (t > 2),
-        "piece": (22.0, 28.0, 30.0, 36.0), "product": (26.1, 28.1, 31.5, 37.0),
-        "add_on": (31.0, 34.0, 36.5, 41.0), "finish": (36.0, 39.0, 42.0, 46.0),
-    },
-)
+ORDER = {
+    "direct": (
+        (3, 5, 15, 25),
+        (92, 101, 111, 119),
+        (182, 189, 199, 207),
+    ),
+    "handed": (
+        (8, 18, 30, 34),
+        (97, 108, 118, 130),
+        (188, 197, 212, 224),
+    ),
+    "split_p": (
+        (14, 21, 35, 39),
+        (98, 113, 127, 138),
+        (191, 202, 218, 229),
+    ),
+    "split_q": (
+        (46, 60, 73, 81),
+        (123, 144, 162, 174),
+        (215, 237, 254, 265),
+    ),
+    "product": (
+        (48, 50, 51, 53, 61, 62, 63, 66, 74, 75, 76, 77, 82, 83, 84, 86),
+        (124, 128, 129, 139, 145, 146, 147, 148, 163, 164, 165, 166, 175, 176, 177, 178),
+        (216, 217, 221, 231, 238, 239, 240, 243, 255, 257, 259, 260, 266, 267, 268, 269),
+    ),
+    "send_out": (
+        (54, 67, 78, 87),
+        (140, 150, 167, 180),
+        (232, 245, 261, 271),
+    ),
+    "add_on": (
+        (64, 79, 90, 91),
+        (156, 161, 179, 183),
+        (249, 252, 272, 273),
+    ),
+    "end": (
+        (71, 89, 94, 96),
+        (171, 172, 185, 193),
+        (263, 270, 274, 275),
+    ),
+    "bc": (
+        (0, 1, 13, 4, 11, 22, 6, 17, 26, 24, 38, 45, 2, 7, 9, 12, 23, 32, 16, 28, 37, 36, 49, 58, 10, 19, 29, 27, 40, 52, 31, 43, 56, 47, 65, 72, 20, 33, 42, 41, 57, 68, 44, 59, 70, 55, 69, 80),
+        (85, 88, 100, 95, 104, 114, 99, 106, 116, 102, 112, 120, 93, 103, 109, 105, 115, 131, 107, 121, 134, 117, 133, 143, 110, 125, 136, 126, 141, 153, 132, 149, 158, 135, 152, 159, 122, 137, 155, 142, 157, 169, 151, 160, 170, 154, 168, 173),
+        (181, 184, 192, 187, 196, 206, 190, 201, 210, 194, 205, 214, 186, 195, 204, 198, 209, 222, 200, 213, 226, 208, 225, 236, 203, 220, 234, 219, 233, 247, 223, 242, 251, 228, 246, 253, 211, 227, 241, 230, 248, 258, 235, 250, 262, 244, 256, 264),
+    ),
+}
 ROLES = (("x", "z", "y"), ("z", "y", "x"), ("y", "x", "z"))
 F32 = jnp.float32
 BF16 = jnp.bfloat16
@@ -190,40 +221,38 @@
             ref = pbuf.at[s, wrap(c + OFFSETS[i]), other, rows(j)]
             rcopy(ref, ref, cx_s.at[s, j, i], cx_r.at[s, j, i], partner).wait_recv()
 
-        def bc_copy(direction, seq, from_root):
-            j = lax.div(seq, 4)
-            part = lax.rem(seq, 4)
-            q = wrap(c + jnp.where(part == 1, -1, jnp.where(part == 2, 1, jnp.where(part == 3, 2, 0))))
-            place = pl.ds(pl.multiple_of(j * CH + direction * HALF, HALF), HALF)
+        def bc_copy(direction, j, i, from_root):
+            q = wrap(c + OFFSETS[i])
+            place = half_rows(j, direction)
             dst = qbuf.at[s, q, place]
             src = pbuf.at[s, q, k, place] if from_root else dst
-            return rcopy(src, dst, bc_s.at[s, direction, seq], bc_r.at[s, direction, seq], at(bn, sign(direction)))
-
-        def bc_root(*seqs):
+            return rcopy(src, dst, bc_s.at[s, direction, j, i], bc_r.at[s, direction, j, i], at(bn, sign(direction)))
+
+        def bc_root(j, *parts):
             @pl.when(root)
             def _():
-                for seq in seqs:
-                    bc_copy(0, jnp.int32(seq), True).start()
-                    bc_copy(1, jnp.int32(seq), True).start()
-
-        def bc_tick(tick):
-            for direction in (0, 1):
-                hops = d - 1 if direction == 0 else 3 - d
-                seq = tick - LAG * hops
-
-                @pl.when(jnp.logical_and(d > 0, jnp.logical_and(seq >= 0, seq < 16)))
-                def _():
-                    copy = bc_copy(direction, seq, False)
+                for i in parts:
+                    bc_copy(0, j, i, True).start()
+                    bc_copy(1, j, i, True).start()
+
+        def bc_hop(hop, j, i):
+            def hand_on(*directions):
+                for direction in directions:
+                    copy = bc_copy(direction, j, i, False)
                     copy.wait_recv()
-
-                    @pl.when(hops < 2)
-                    def _():
+                    if hop < 3:
                         copy.start()
+
+            if hop == 2:
+                pl.when(d == 2)(functools.partial(hand_on, 0, 1))
+            else:
+                pl.when(d == hop)(functools.partial(hand_on, 0))
+                pl.when(d == 4 - hop)(functools.partial(hand_on, 1))
 
         def ready(j):
             ag_copy(0, j).start()
             ag_copy(1, j).start()
-            bc_root(4 * j)
+            bc_root(j, 0)
             cx_copy(j, 0).start()
 
         def direct(j):
@@ -234,13 +263,13 @@
                 ready(j + 2)
             cx_copy(j, 1).start()
             cx_copy(j, 2).start()
-            bc_root(4 * j + 1, 4 * j + 2)
+            bc_root(j, 1, 2)
 
         def handed(j):
             for direction in (0, 1):
                 af_wait(direction, j)
             cx_copy(j, 3).start()
-            bc_root(4 * j + 3)
+            bc_root(j, 3)
 
         def split_p(j):
             for i in range(4):
@@ -343,8 +372,9 @@
 
                 @pl.when(d != (3 if direction == 0 else 1))
                 def _():
-                    for seq in range(16):
-                        bc_copy(direction, jnp.int32(seq), False).wait_send()
+                    for j in range(4):
+                        for i in range(4):
+                            bc_copy(direction, j, i, False).wait_send()
             for j in range(4):
                 for i in range(4):
                     cx_copy(j, i).wait_send()
@@ -379,50 +409,56 @@
             steps[s + 1]["ready"](j)
 
     call = functools.partial
+    units = range(4)
+    hops = (1, 2, 3)
     for s in range(STEPS):
         now = steps[s]
-        zero = START_AT[s]
-        plan = ARRIVE[min(s, 1)]
-        for j in range(4):
+
+        def place(kind, n):
+            return ORDER[kind][s][n]
+
+        for j in units:
             begun = [("end", s - 1, j)] if s else []
-            due(("direct", s, j), zero + plan["direct"][j], call(now["direct"], j), begun)
-            due(("handed", s, j), zero + plan["handed"][j], call(now["handed"], j), [("direct", s, j)])
-            due(("split_p", s, j), zero + plan["split_p"][j], call(now["split_p"], j), [("handed", s, j)])
-        tick = plan["tick"]
-        for t in range(16 + 2 * LAG):
-            due(("tick", s, t), zero + tick(t), call(now["bc_tick"], t), [("tick", s, t - 1)] if t else begun)
+            due(("direct", s, j), place("direct", j), call(now["direct"], j), begun)
+            due(("handed", s, j), place("handed", j), call(now["handed"], j), [("direct", s, j)])
+            due(("split_p", s, j), place("split_p", j), call(now["split_p"], j), [("handed", s, j)])
+            for i in units:
+                first = begun if i == 0 else [("handed" if i == 3 else "direct", s, j)]
+                for hop in hops:
+                    needs = [("bc", s, j, i, hop - 1)] if hop > 1 else first
+                    due(("bc", s, j, i, hop), place("bc", j * 12 + i * 3 + hop - 1), call(now["bc_hop"], hop, j, i), needs)
         if s < 2:
-            due(("mask", s), zero + 13.0, now["mask"], [("end", s - 1, 3)] if s else [])
-        for j in range(4):
-            due(("split_q", s, j), zero + plan["piece"][j], call(now["split_q"], j),
-                [("tick", s, 4 * j + 3 + 2 * LAG), ("handed", s, j)])
-            early = 3 if j == 0 else 0
-            if early:
-                due(("early", s, j), zero + plan["piece"][j], call(now["product"], j, 0, early),
-                    [("split_q", s, j), ("split_p", s, early - 1)])
-            due(("product", s, j), zero + plan["product"][j], call(now["product"], j, early, 4),
-                [("split_q", s, j), ("split_p", s, 3)] + ([("early", s, j)] if early else []))
-            due(("send_out", s, j), zero + plan["product"][j], call(now["send_out"], j), [("product", s, j)])
-            due(("add_on", s, j), zero + plan["add_on"][j], call(now["add_on"], j), [("send_out", s, j)])
-            due(("end", s, j), zero + plan["finish"][j], call(end_unit, s, j),
+            due(("mask", s), place("direct", 3), now["mask"], [("direct", s, 3)])
+        for j in units:
+            due(("split_q", s, j), place("split_q", j), call(now["split_q"], j),
+                [("bc", s, j, i, hop) for i in units for hop in hops] + [("handed", s, j)])
+            before = ("split_q", s, j)
+            for n in units:
+                due(("product", s, j, n), place("product", j * 4 + n), call(now["product"], j, n, n + 1),
+                    [before, ("split_p", s, n)])
+                before = ("product", s, j, n)
+            due(("send_out", s, j), place("send_out", j), call(now["send_out"], j), [before])
+            due(("add_on", s, j), place("add_on", j), call(now["add_on"], j), [("send_out", s, j)])
+            due(("end", s, j), place("end", j), call(end_unit, s, j),
                 [("add_on", s, j)] + ([("mask", s)] if s < 2 else []))
-        due(("sum", s), zero + plan["sum"], call(square_sum, s, now["c"]), [("end", s - 1, 3)] if s else [])
+        late = [("end", s - 1, n) for n in units] if s else []
+        due(("sum", s), place("direct", 2), call(square_sum, s, now["c"]), late)
         if s > 0:
-            due(("sent", s - 1), zero + 16.0, steps[s - 1]["sent"], [("end", s - 1, 3)])
-            due(("rs_sent", s - 1), zero + 20.0, steps[s - 1]["rs_sent"], [("end", s - 1, 3)])
+            due(("sent", s - 1), place("handed", 2), steps[s - 1]["sent"], late + [("direct", s, 3)])
+            due(("rs_sent", s - 1), place("handed", 3), steps[s - 1]["rs_sent"], late + [("direct", s, 3)])
         if s == 2:
             chain = [
-                (0.0, lambda: trace_core().start()),
-                (17.0, trace_core_end), (17.0, call(trace_axis_start, 1, "x")),
-                (22.0, call(trace_axis_end, 1, "x")), (22.0, call(trace_axis_start, 2, "y")),
-                (29.0, call(trace_axis_end, 2, "y")), (29.0, call(trace_axis_start, 3, "z")),
-                (38.0, call(trace_axis_end, 3, "z")),
+                (place("direct", 2), lambda: trace_core().start()),
+                (place("handed", 2), trace_core_end), (place("handed", 2), call(trace_axis_start, 1, "x")),
+                (place("split_p", 3), call(trace_axis_end, 1, "x")), (place("split_p", 3), call(trace_axis_start, 2, "y")),
+                (place("send_out", 2), call(trace_axis_end, 2, "y")), (place("send_out", 2), call(trace_axis_start, 3, "z")),
+                (place("add_on", 3), call(trace_axis_end, 3, "z")),
             ]
             before = ("sum", 2)
             for n, (time, act) in enumerate(chain):
-                due(("trace", n), zero + time, act, [before])
+                due(("trace", n), time, act, [before])
                 before = ("trace", n)
-            due(("sent", s), zero + 39.0, now["sent"], [("tick", s, 15 + 2 * LAG), ("handed", s, 3)])
+            due(("sent", s), place("add_on", 3), now["sent"], [("split_q", s, j) for j in units])
     for _, _, act in sorted(events.values(), key=lambda event: event[:2]):
         act()
     tr_out[...] = vsend[4]
@@ -479,7 +515,7 @@
             dma((STEPS, 2, 4)), dma((STEPS, 2, 4)),
             dma((STEPS, 2, 4)), dma((STEPS, 2, 4)),
             dma((STEPS, 4, 4)), dma((STEPS, 4, 4)),
-            dma((STEPS, 2, 16)), dma((STEPS, 2, 16)),
+            dma((STEPS, 2, 4, 4)), dma((STEPS, 2, 4, 4)),
             dma((STEPS, 2, 4, 3)), dma((STEPS, 2, 4, 3)),
             dma((2, 4)), dma((2, 4)),
             dma((4, 4)), dma((4, 4)),

time: 171 us -> 159 us (0.930)
  Pallas kernels: 164 us -> 151 us
    pallas_call x1, Pallas kernels: 164 us -> 151 us  [per_device(): pl.pallas_call(body, out_shape=(jax.ShapeDtypeStruct((BLK, 256), F32), ja...]
where the time goes in v3:
time: 159 us; the launch traced here: 157 us
  Pallas kernels  151 us (95%)
  local copies, waits for them, and re-layouts  4.92 us (3%)
    pallas_call x1, Pallas kernels, per_device(): pl.pallas_call(body, out_shape=(jax.ShapeDtypeStruct((BLK, 256), F32), ja...  151 us
    unnamed x2, local copies, waits for them, and re-layouts  3.62 us

profile of v3, /device:TPU:37, one launch (start us, length us, event | category | flops | bytes accessed | tf_op | source)
XLA Modules:
  0.0 156.6 jit_solution(16150666042898122745)
XLA Ops:
  0.6 1.4 copy.6.pat
  2.0 151.0 %purify.1 = (f32[1024,256]{1,0:T(8,128)}, f32[8,128]{1,0:T(8,128)}) custom-call(f32[1024,256]{1,0:T(8,128)} %dens.1, s32[16,4]{1,0:T(8,128)} %copy.6.pat, s32[3]{0:T(128)} %br.1), custom_call_target="tpu_custom_call" | custom-call | tf_op jit(solution)/shard_map/purify/pallas_call | solution.py:491
  153.0 1.3 slice_reduce_fusion
  154.3 2.3 %copy.8 = f32[1024,256]{1,0:T(8,128)} copy(f32[1024,256]{1,0:T(8,128)} %get-tuple-element.8) | data formatting | bytes 2097152

commit v4 on v3

--- a/solution.py
+++ b/solution.py
@@ -16,50 +16,55 @@
 HALF = 16
 OFFSETS = (0, -1, 1, 2)
 ORDER = {
+    "ready": (
+        (),
+        (78, 100, 109, 112),
+        (196, 199, 221, 228),
+    ),
     "direct": (
-        (3, 5, 15, 25),
-        (92, 101, 111, 119),
-        (182, 189, 199, 207),
+        (3, 4, 6, 7, 16, 17, 27, 28),
+        (106, 107, 115, 119, 129, 126, 138, 140),
+        (213, 211, 215, 214, 236, 237, 244, 245),
     ),
     "handed": (
-        (8, 18, 30, 34),
-        (97, 108, 118, 130),
-        (188, 197, 212, 224),
+        (10, 22, 38, 39),
+        (113, 131, 134, 151),
+        (223, 226, 253, 259),
     ),
     "split_p": (
-        (14, 21, 35, 39),
-        (98, 113, 127, 138),
-        (191, 202, 218, 229),
+        (19, 30, 42, 47),
+        (116, 132, 142, 158),
+        (232, 242, 260, 268),
     ),
     "split_q": (
-        (46, 60, 73, 81),
-        (123, 144, 162, 174),
-        (215, 237, 254, 265),
+        (50, 64, 83, 85),
+        (147, 166, 186, 204),
+        (250, 273, 292, 305),
     ),
     "product": (
-        (48, 50, 51, 53, 61, 62, 63, 66, 74, 75, 76, 77, 82, 83, 84, 86),
-        (124, 128, 129, 139, 145, 146, 147, 148, 163, 164, 165, 166, 175, 176, 177, 178),
-        (216, 217, 221, 231, 238, 239, 240, 243, 255, 257, 259, 260, 266, 267, 268, 269),
+        (51, 53, 54, 55, 65, 66, 67, 71, 92, 93, 94, 95, 86, 87, 88, 89),
+        (148, 149, 150, 159, 167, 168, 169, 170, 187, 188, 189, 190, 205, 206, 207, 208),
+        (251, 252, 261, 269, 276, 277, 280, 282, 293, 295, 299, 300, 306, 307, 308, 309),
     ),
     "send_out": (
-        (54, 67, 78, 87),
-        (140, 150, 167, 180),
-        (232, 245, 261, 271),
+        (56, 57, 72, 73, 96, 97, 91, 90),
+        (160, 161, 172, 177, 191, 192, 209, 210),
+        (270, 271, 283, 284, 301, 302, 310, 311),
     ),
     "add_on": (
-        (64, 79, 90, 91),
-        (156, 161, 179, 183),
-        (249, 252, 272, 273),
+        (68, 69, 79, 80, 103, 102, 104, 105),
+        (178, 180, 182, 183, 201, 202, 217, 218),
+        (288, 287, 296, 298, 313, 312, 315, 316),
     ),
     "end": (
-        (71, 89, 94, 96),
-        (171, 172, 185, 193),
-        (263, 270, 274, 275),
+        (77, 99, 108, 111),
+        (195, 198, 220, 227),
+        (314, 317, 318, 319),
     ),
     "bc": (
-        (0, 1, 13, 4, 11, 22, 6, 17, 26, 24, 38, 45, 2, 7, 9, 12, 23, 32, 16, 28, 37, 36, 49, 58, 10, 19, 29, 27, 40, 52, 31, 43, 56, 47, 65, 72, 20, 33, 42, 41, 57, 68, 44, 59, 70, 55, 69, 80),
-        (85, 88, 100, 95, 104, 114, 99, 106, 116, 102, 112, 120, 93, 103, 109, 105, 115, 131, 107, 121, 134, 117, 133, 143, 110, 125, 136, 126, 141, 153, 132, 149, 158, 135, 152, 159, 122, 137, 155, 142, 157, 169, 151, 160, 170, 154, 168, 173),
-        (181, 184, 192, 187, 196, 206, 190, 201, 210, 194, 205, 214, 186, 195, 204, 198, 209, 222, 200, 213, 226, 208, 225, 236, 203, 220, 234, 219, 233, 247, 223, 242, 251, 228, 246, 253, 211, 227, 241, 230, 248, 258, 235, 250, 262, 244, 256, 264),
+        (0, 2, 15, 5, 11, 25, 8, 20, 33, 23, 40, 49, 1, 9, 18, 13, 26, 37, 14, 29, 41, 35, 52, 63, 12, 24, 34, 31, 44, 82, 32, 48, 60, 58, 70, 81, 21, 36, 46, 43, 61, 75, 45, 62, 76, 59, 74, 84),
+        (98, 101, 118, 114, 123, 135, 117, 128, 136, 120, 130, 143, 110, 121, 124, 122, 133, 146, 125, 141, 154, 139, 153, 165, 127, 145, 157, 144, 162, 175, 152, 171, 181, 155, 174, 184, 137, 156, 176, 163, 179, 194, 164, 193, 197, 173, 185, 203),
+        (200, 212, 225, 219, 230, 240, 224, 234, 241, 229, 239, 249, 216, 222, 233, 231, 243, 256, 235, 248, 264, 246, 258, 272, 238, 254, 267, 255, 266, 285, 257, 275, 290, 263, 281, 291, 247, 262, 279, 265, 286, 297, 274, 289, 303, 278, 294, 304),
     ),
 }
 ROLES = (("x", "z", "y"), ("z", "y", "x"), ("y", "x", "z"))
@@ -82,8 +87,8 @@
 
 
 def body(
-    dens, pat, br, out, tr_out,
-    pbuf, qbuf, phi, plo, qcat, obuf, r1, r2, patf, gbuf, mbuf, vsend, vcore, vaxis, fin,
+    dens, pat, br, fin_out, tr_out, pat_out,
+    pbuf, qbuf, phi, plo, qcat, obuf, r1, r2, patf, gbuf, mbuf, vsend, vcore, vaxis, fin, wide,
     ag_s, ag_r, af_s, af_r, cx_s, cx_r, bc_s, bc_r, rs_s, rs_r, pt_s, pt_r, tr_s, tr_r, fx_s, fx_r,
 ):
     col = lax.axis_index("col")
@@ -124,9 +129,10 @@
         mine = pl.ds(pl.multiple_of(k * 128, 128), 128)
         piece = jnp.concatenate([dens[row:row + CH, mine] for row in lane_rows(i)], axis=0)
         pbuf[0, pos["y"], k, :, i * 128:(i + 1) * 128] = piece.T
-    patf[...] = jnp.zeros_like(patf)
     vsend[0] = jnp.zeros((8, 128), F32)
-    patf[:, 0:4] = pat[...].astype(F32)
+    wide[...] = jnp.zeros_like(wide)
+    wide[0:4, 0:16] = pat[...].astype(F32)
+    patf[...] = wide[...].T[0:16, :]
     pl.semaphore_wait(barrier, len(greet))
 
     def pattern_copies():
@@ -255,15 +261,13 @@
             bc_root(j, 0)
             cx_copy(j, 0).start()
 
-        def direct(j):
-            for direction in (0, 1):
-                ag_wait(direction, j)
-                af_copy(direction, j).start()
-            if s == 0 and j < 2:
+        def direct(j, direction):
+            ag_wait(direction, j)
+            af_copy(direction, j).start()
+            if s == 0 and j < 2 and direction == 1:
                 ready(j + 2)
-            cx_copy(j, 1).start()
-            cx_copy(j, 2).start()
-            bc_root(j, 1, 2)
+            cx_copy(j, 1 + direction).start()
+            bc_root(j, 1 + direction)
 
         def handed(j):
             for direction in (0, 1):
@@ -310,10 +314,9 @@
                 same = qcat[j, :SLAB, lanes].astype(F32) + qcat[j, SLAB:, lanes].astype(F32)
                 obuf[s, j, :, lanes] = scale * value + linear * same
 
-        def send_out(j):
-            for i in (0, 1):
-                for direction in (0, 1):
-                    rs_copy(direction, i, j).start()
+        def send_out(j, i):
+            for direction in (0, 1):
+                rs_copy(direction, i, j).start()
 
         def out_half(q, second):
             return pl.ds(pl.multiple_of(q * CH + second * HALF, HALF), HALF)
@@ -328,12 +331,11 @@
                 dst = r2.at[s, direction, j, pl.ds(second * HALF, HALF)]
             return rcopy(src, dst, rs_s.at[s, direction, j, i], rs_r.at[s, direction, j, i], at(an, sign(direction)))
 
-        def add_on(j):
-            for direction in (0, 1):
-                rs_copy(direction, 0, j).wait_recv()
-                place = out_half(up if direction == 0 else down, direction)
-                obuf[s, j, place, :] = obuf[s, j, place, :] + r1[s, direction, j]
-                rs_copy(direction, 2, j).start()
+        def add_on(j, direction):
+            rs_copy(direction, 0, j).wait_recv()
+            place = out_half(up if direction == 0 else down, direction)
+            obuf[s, j, place, :] = obuf[s, j, place, :] + r1[s, direction, j]
+            rs_copy(direction, 2, j).start()
 
         def mask():
             pattern_wait(s)
@@ -403,11 +405,6 @@
         time = max([time] + [events[need][0] for need in needs])
         events[name] = (time, len(events), act)
 
-    def end_unit(s, j):
-        steps[s]["finish"](j)
-        if s + 1 < STEPS:
-            steps[s + 1]["ready"](j)
-
     call = functools.partial
     units = range(4)
     hops = (1, 2, 3)
@@ -418,17 +415,21 @@
             return ORDER[kind][s][n]
 
         for j in units:
-            begun = [("end", s - 1, j)] if s else []
-            due(("direct", s, j), place("direct", j), call(now["direct"], j), begun)
-            due(("handed", s, j), place("handed", j), call(now["handed"], j), [("direct", s, j)])
+            begun = [("direct", 0, j - 2, 1)] if j > 1 else []
+            if s:
+                due(("ready", s, j), place("ready", j), call(now["ready"], j), [("end", s - 1, j)])
+                begun = [("ready", s, j)]
+            for n in (0, 1):
+                due(("direct", s, j, n), place("direct", 2 * j + n), call(now["direct"], j, n), begun)
+            due(("handed", s, j), place("handed", j), call(now["handed"], j), [("direct", s, j, 0), ("direct", s, j, 1)])
             due(("split_p", s, j), place("split_p", j), call(now["split_p"], j), [("handed", s, j)])
+            starts = (begun, [("direct", s, j, 0)], [("direct", s, j, 1)], [("handed", s, j)])
             for i in units:
-                first = begun if i == 0 else [("handed" if i == 3 else "direct", s, j)]
                 for hop in hops:
-                    needs = [("bc", s, j, i, hop - 1)] if hop > 1 else first
+                    needs = [("bc", s, j, i, hop - 1)] if hop > 1 else starts[i]
                     due(("bc", s, j, i, hop), place("bc", j * 12 + i * 3 + hop - 1), call(now["bc_hop"], hop, j, i), needs)
         if s < 2:
-            due(("mask", s), place("direct", 3), now["mask"], [("direct", s, 3)])
+            due(("mask", s), place("direct", 7), now["mask"], [("direct", s, 3, 1)])
         for j in units:
             due(("split_q", s, j), place("split_q", j), call(now["split_q"], j),
                 [("bc", s, j, i, hop) for i in units for hop in hops] + [("handed", s, j)])
@@ -437,65 +438,75 @@
                 due(("product", s, j, n), place("product", j * 4 + n), call(now["product"], j, n, n + 1),
                     [before, ("split_p", s, n)])
                 before = ("product", s, j, n)
-            due(("send_out", s, j), place("send_out", j), call(now["send_out"], j), [before])
-            due(("add_on", s, j), place("add_on", j), call(now["add_on"], j), [("send_out", s, j)])
-            due(("end", s, j), place("end", j), call(end_unit, s, j),
-                [("add_on", s, j)] + ([("mask", s)] if s < 2 else []))
+            for n in (0, 1):
+                due(("send_out", s, j, n), place("send_out", 2 * j + n), call(now["send_out"], j, n), [before])
+            for n in (0, 1):
+                due(("add_on", s, j, n), place("add_on", 2 * j + n), call(now["add_on"], j, n), [("send_out", s, j, 0)])
+            due(("end", s, j), place("end", j), call(now["finish"], j),
+                [("add_on", s, j, 0), ("add_on", s, j, 1), ("send_out", s, j, 1)] + ([("mask", s)] if s < 2 else []))
         late = [("end", s - 1, n) for n in units] if s else []
-        due(("sum", s), place("direct", 2), call(square_sum, s, now["c"]), late)
+        due(("sum", s), place("direct", 5), call(square_sum, s, now["c"]), late)
         if s > 0:
-            due(("sent", s - 1), place("handed", 2), steps[s - 1]["sent"], late + [("direct", s, 3)])
-            due(("rs_sent", s - 1), place("handed", 3), steps[s - 1]["rs_sent"], late + [("direct", s, 3)])
+            due(("sent", s - 1), place("handed", 2), steps[s - 1]["sent"], late + [("direct", s, 3, 0), ("direct", s, 3, 1)])
+            due(("rs_sent", s - 1), place("handed", 3), steps[s - 1]["rs_sent"], late + [("direct", s, 3, 0), ("direct", s, 3, 1)])
         if s == 2:
             chain = [
-                (place("direct", 2), lambda: trace_core().start()),
+                (place("direct", 5), lambda: trace_core().start()),
                 (place("handed", 2), trace_core_end), (place("handed", 2), call(trace_axis_start, 1, "x")),
                 (place("split_p", 3), call(trace_axis_end, 1, "x")), (place("split_p", 3), call(trace_axis_start, 2, "y")),
-                (place("send_out", 2), call(trace_axis_end, 2, "y")), (place("send_out", 2), call(trace_axis_start, 3, "z")),
-                (place("add_on", 3), call(trace_axis_end, 3, "z")),
+                (place("send_out", 5), call(trace_axis_end, 2, "y")), (place("send_out", 5), call(trace_axis_start, 3, "z")),
+                (place("add_on", 7), call(trace_axis_end, 3, "z")),
             ]
             before = ("sum", 2)
             for n, (time, act) in enumerate(chain):
                 due(("trace", n), time, act, [before])
                 before = ("trace", n)
-            due(("sent", s), place("add_on", 3), now["sent"], [("split_q", s, j) for j in units])
+            due(("sent", s), place("add_on", 7), now["sent"], [("split_q", s, j) for j in units])
     for _, _, act in sorted(events.values(), key=lambda event: event[:2]):
         act()
     tr_out[...] = vsend[4]
+    pat_out[...] = patf[...]
+    steps[2]["rs_sent"]()
+    for j in range(4):
+        fin_copy(j, other).wait_recv()
+    for j in range(4):
+        fin_copy(j, k).wait_send()
+    fin_out[...] = fin[...]
+
+
+def place_body(fin, pat, totals, out, traces):
     left = lax.broadcasted_iota(jnp.int32, (128, 256), 0)
     right = lax.broadcasted_iota(jnp.int32, (128, 256), 1)
     spread = (left == right // BS).astype(F32)
     line = lax.broadcasted_iota(jnp.int32, (128, 16), 0)
     block = lax.broadcasted_iota(jnp.int32, (128, 16), 1)
-    steps[2]["rs_sent"]()
-    for j in range(4):
-        fin_copy(j, other).wait_recv()
     for i in range(8):
         here = [line // CH == n for n in range(4)]
         wanted = sum(jnp.where(here[n], row // BS, 0) for n, row in enumerate(lane_rows(i)))
         pick = (block == wanted).astype(F32)
-        chosen = jnp.dot(pick, patf[...], preferred_element_type=F32)
+        chosen = jnp.dot(pick, pat[...], preferred_element_type=F32)
         mask = jnp.dot(chosen, spread, preferred_element_type=F32)
         for half in range(2):
             lanes = slice(half * 128, (half + 1) * 128)
             part = fin[half, :, i * 128:(i + 1) * 128].T * mask[:, lanes]
             for n, row in enumerate(lane_rows(i)):
                 out[row:row + CH, lanes] = part[n * CH:(n + 1) * CH]
-    for j in range(4):
-        fin_copy(j, k).wait_send()
+    for i in range(STEPS):
+        traces[i] = totals[i, 0]
 
 
 def per_device(density, pattern, branches):
     vmem = pl.BlockSpec(memory_space=pltpu.VMEM)
     dma = pltpu.SemaphoreType.DMA
-    purified, traces = pl.pallas_call(
+    last, totals, kept = pl.pallas_call(
         body,
         out_shape=(
-            jax.ShapeDtypeStruct((BLK, 256), F32),
+            jax.ShapeDtypeStruct((2, SLAB, BLK), F32),
             jax.ShapeDtypeStruct((8, 128), F32),
+            jax.ShapeDtypeStruct((16, 128), F32),
         ),
         in_specs=[vmem, vmem, pl.BlockSpec(memory_space=pltpu.SMEM)],
-        out_specs=(vmem, vmem),
+        out_specs=(vmem, vmem, vmem),
         scratch_shapes=[
             pltpu.VMEM((STEPS, 4, 2, SLAB, BLK), F32),
             pltpu.VMEM((STEPS, 4, SLAB, BLK), F32),
@@ -512,6 +523,7 @@
             pltpu.VMEM((8, 128), F32),
             pltpu.VMEM((4, 4, 8, 128), F32),
             pltpu.VMEM((2, SLAB, BLK), F32),
+            pltpu.VMEM((128, 128), F32),
             dma((STEPS, 2, 4)), dma((STEPS, 2, 4)),
             dma((STEPS, 2, 4)), dma((STEPS, 2, 4)),
             dma((STEPS, 4, 4)), dma((STEPS, 4, 4)),
@@ -525,8 +537,15 @@
             collective_id=0, has_side_effects=True, vmem_limit_bytes=56 * 2**20
         ),
         name="purify",
-    )(density, pattern, branches)
-    return purified, traces[:STEPS, 0]
+    )(density, pattern.T, branches)
+    smem = pl.BlockSpec(memory_space=pltpu.SMEM)
+    return pl.pallas_call(
+        place_body,
+        out_shape=(jax.ShapeDtypeStruct((BLK, 256), F32), jax.ShapeDtypeStruct((STEPS,), F32)),
+        in_specs=[vmem, vmem, smem],
+        out_specs=(vmem, smem),
+        name="place",
+    )(last, kept, totals)
 
 
 def solution(mesh):

time: 159 us -> 155 us (0.975)
  local copies, waits for them, and re-layouts: 4.92 us -> 0 us
    unnamed x2 -> x0, local copies, waits for them, and re-layouts: 3.62 us -> none
    pallas_call x1 -> x2, Pallas kernels: 151 us -> 152 us  [the longest x1 149 us: per_device(): pl.pallas_call(body, out_shape=(jax.ShapeDtypeStruct((2, SLAB, BLK), F32)...]
where the time goes in v4:
time: 155 us; the launch traced here: 153 us
  Pallas kernels  152 us (98%)
    pallas_call x1, Pallas kernels, per_device(): pl.pallas_call(body, out_shape=(jax.ShapeDtypeStruct((2, SLAB, BLK), F32)...  149 us

profile of v4, /device:TPU:37, one launch (start us, length us, event | category | flops | bytes accessed | tf_op | source)
XLA Modules:
  0.0 153.0 jit_solution(13047287604576395908)
XLA Ops:
  0.6 149.2 %purify.1 = (f32[2,128,1024]{2,1,0:T(8,128)}, f32[8,128]{1,0:T(8,128)}, f32[16,128]{1,0:T(8,128)}) custom-call(f32[1024,256]{1,0:T(8,128)} %dens.1, s32[4,16]{1,0:T(4,128)} %bitcast.1, s32[3]{0:T(128)} %br.1), custom_call_target="tpu_custom_call" | custom-call | tf_op jit(solution)/shard_map/purify/pallas_call | solution.py:501
  149.9 3.0 %place.1 = (f32[1024,256]{1,0:T(8,128)}, f32[3]{0:T(128)}) custom-call(f32[2,128,1024]{2,1,0:T(8,128)} %get-tuple-element.5.fin, f32[16,128]{1,0:T(8,128)} %get-tuple-element.6.pat, f32[8,128]{1,0:T(8,128)} %get-tuple-element.7.totals), custom_call_target="tpu_custom_call" | custom-call | tf_op jit(solution)/shard_map/place/pallas_call | solution.py:542

commit v5 on v4

--- a/solution.py
+++ b/solution.py
@@ -89,7 +89,7 @@
 def body(
     dens, pat, br, fin_out, tr_out, pat_out,
     pbuf, qbuf, phi, plo, qcat, obuf, r1, r2, patf, gbuf, mbuf, vsend, vcore, vaxis, fin, wide,
-    ag_s, ag_r, af_s, af_r, cx_s, cx_r, bc_s, bc_r, rs_s, rs_r, pt_s, pt_r, tr_s, tr_r, fx_s, fx_r,
+    ag_s, ag_r, af_r, cx_s, cx_r, bc_s, bc_r, rs_s, rs_r, pt_s, pt_r, tr_s, tr_r, fx_s, fx_r,
 ):
     col = lax.axis_index("col")
     k = lax.axis_index("depth")
@@ -205,34 +205,34 @@
 
         def ag_copy(direction, j):
             ref = pbuf.at[s, c, k, rows(j)]
-            return rcopy(ref, ref, ag_s.at[s, direction, j], ag_r.at[s, direction, j], at(cn, sign(direction)))
+            return rcopy(ref, ref, ag_s.at[s, direction], ag_r.at[s, direction, j], at(cn, sign(direction)))
 
         def ag_wait(direction, j):
             ref = pbuf.at[s, wrap(c - sign(direction)), k, rows(j)]
-            rcopy(ref, ref, ag_s.at[s, direction, j], ag_r.at[s, direction, j], partner).wait_recv()
+            rcopy(ref, ref, ag_s.at[s, direction], ag_r.at[s, direction, j], partner).wait_recv()
 
         def af_copy(direction, j):
             ref = pbuf.at[s, wrap(c - sign(direction)), k, half_rows(j, direction)]
-            return rcopy(ref, ref, af_s.at[s, direction, j], af_r.at[s, direction, j], at(cn, sign(direction)))
+            return rcopy(ref, ref, ag_s.at[s, direction], af_r.at[s, direction, j], at(cn, sign(direction)))
 
         def af_wait(direction, j):
             ref = pbuf.at[s, wrap(c + 2), k, half_rows(j, direction)]
-            rcopy(ref, ref, af_s.at[s, direction, j], af_r.at[s, direction, j], partner).wait_recv()
+            rcopy(ref, ref, ag_s.at[s, direction], af_r.at[s, direction, j], partner).wait_recv()
 
         def cx_copy(j, i):
             ref = pbuf.at[s, wrap(c + OFFSETS[i]), k, rows(j)]
-            return rcopy(ref, ref, cx_s.at[s, j, i], cx_r.at[s, j, i], partner)
+            return rcopy(ref, ref, cx_s.at[s], cx_r.at[s, j, i], partner)
 
         def cx_wait(j, i):
             ref = pbuf.at[s, wrap(c + OFFSETS[i]), other, rows(j)]
-            rcopy(ref, ref, cx_s.at[s, j, i], cx_r.at[s, j, i], partner).wait_recv()
+            rcopy(ref, ref, cx_s.at[s], cx_r.at[s, j, i], partner).wait_recv()
 
         def bc_copy(direction, j, i, from_root):
             q = wrap(c + OFFSETS[i])
             place = half_rows(j, direction)
             dst = qbuf.at[s, q, place]
             src = pbuf.at[s, q, k, place] if from_root else dst
-            return rcopy(src, dst, bc_s.at[s, direction, j, i], bc_r.at[s, direction, j, i], at(bn, sign(direction)))
+            return rcopy(src, dst, bc_s.at[s, direction], bc_r.at[s, direction, j, i], at(bn, sign(direction)))
 
         def bc_root(j, *parts):
             @pl.when(root)
@@ -329,7 +329,7 @@
                 second = 1 - direction if i == 1 else direction
                 src = obuf.at[s, j, out_half(near, second)]
                 dst = r2.at[s, direction, j, pl.ds(second * HALF, HALF)]
-            return rcopy(src, dst, rs_s.at[s, direction, j, i], rs_r.at[s, direction, j, i], at(an, sign(direction)))
+            return rcopy(src, dst, rs_s.at[s, direction], rs_r.at[s, direction, j, i], at(an, sign(direction)))
 
         def add_on(j, direction):
             rs_copy(direction, 0, j).wait_recv()
@@ -366,29 +366,24 @@
                 fin[k, rows(j), :] = value
                 fin_copy(j, k).start()
 
+        def all_sent(ref, send, recv):
+            rcopy(ref, ref, send, recv, partner).wait_send()
+
         def sent():
             for direction in (0, 1):
-                for j in range(4):
-                    ag_copy(direction, j).wait_send()
-                    af_copy(direction, j).wait_send()
+                all_sent(pbuf.at[s, 0, :, pl.ds(0, 96)], ag_s.at[s, direction], ag_r.at[s, direction, 0])
 
                 @pl.when(d != (3 if direction == 0 else 1))
                 def _():
-                    for j in range(4):
-                        for i in range(4):
-                            bc_copy(direction, j, i, False).wait_send()
-            for j in range(4):
-                for i in range(4):
-                    cx_copy(j, i).wait_send()
+                    all_sent(qbuf.at[s, pl.ds(0, 2)], bc_s.at[s, direction], bc_r.at[s, direction, 0, 0])
+            all_sent(qbuf.at[s], cx_s.at[s], cx_r.at[s, 0, 0])
             if s == 0:
                 for copy in pattern_copies():
                     copy.wait_send()
 
         def rs_sent():
             for direction in (0, 1):
-                for j in range(4):
-                    for i in range(3):
-                        rs_copy(direction, i, j).wait_send()
+                all_sent(obuf.at[s, pl.ds(0, 2), pl.ds(0, 96)], rs_s.at[s, direction], rs_r.at[s, direction, 0, 0])
 
         step.update(locals())
         return step
@@ -524,11 +519,10 @@
             pltpu.VMEM((4, 4, 8, 128), F32),
             pltpu.VMEM((2, SLAB, BLK), F32),
             pltpu.VMEM((128, 128), F32),
-            dma((STEPS, 2, 4)), dma((STEPS, 2, 4)),
-            dma((STEPS, 2, 4)), dma((STEPS, 2, 4)),
-            dma((STEPS, 4, 4)), dma((STEPS, 4, 4)),
-            dma((STEPS, 2, 4, 4)), dma((STEPS, 2, 4, 4)),
-            dma((STEPS, 2, 4, 3)), dma((STEPS, 2, 4, 3)),
+            dma((STEPS, 2)), dma((STEPS, 2, 4)), dma((STEPS, 2, 4)),
+            dma((STEPS,)), dma((STEPS, 4, 4)),
+            dma((STEPS, 2)), dma((STEPS, 2, 4, 4)),
+            dma((STEPS, 2)), dma((STEPS, 2, 4, 3)),
             dma((2, 4)), dma((2, 4)),
             dma((4, 4)), dma((4, 4)),
             dma((4,)), dma((4,)),

time: 155 us -> 153 us (0.987)
  Pallas kernels: 152 us -> 150 us
    pallas_call x1, Pallas kernels: 149 us -> 147 us  [per_device(): pl.pallas_call(body, out_shape=(jax.ShapeDtypeStruct((2, SLAB, BLK), F32)...]
where the time goes in v5:
time: 153 us; the launch traced here: 151 us
  Pallas kernels  150 us (98%)
    pallas_call x1, Pallas kernels, per_device(): pl.pallas_call(body, out_shape=(jax.ShapeDtypeStruct((2, SLAB, BLK), F32)...  147 us

profile of v5, /device:TPU:37, one launch (start us, length us, event | category | flops | bytes accessed | tf_op | source)
XLA Modules:
  0.0 150.7 jit_solution(4124845042359721496)
XLA Ops:
  0.6 146.9 %purify.1 = (f32[2,128,1024]{2,1,0:T(8,128)}, f32[8,128]{1,0:T(8,128)}, f32[16,128]{1,0:T(8,128)}) custom-call(f32[1024,256]{1,0:T(8,128)} %dens.1, s32[4,16]{1,0:T(4,128)} %bitcast.1, s32[3]{0:T(128)} %br.1), custom_call_target="tpu_custom_call" | custom-call | tf_op jit(solution)/shard_map/purify/pallas_call | solution.py:496
  147.6 3.0 %place.1 = (f32[1024,256]{1,0:T(8,128)}, f32[3]{0:T(128)}) custom-call(f32[2,128,1024]{2,1,0:T(8,128)} %get-tuple-element.5.fin, f32[16,128]{1,0:T(8,128)} %get-tuple-element.6.pat, f32[8,128]{1,0:T(8,128)} %get-tuple-element.7.totals), custom_call_target="tpu_custom_call" | custom-call | tf_op jit(solution)/shard_map/place/pallas_call | solution.py:536

commit v6 on v5

--- a/solution.py
+++ b/solution.py
@@ -424,7 +424,7 @@
                     needs = [("bc", s, j, i, hop - 1)] if hop > 1 else starts[i]
                     due(("bc", s, j, i, hop), place("bc", j * 12 + i * 3 + hop - 1), call(now["bc_hop"], hop, j, i), needs)
         if s < 2:
-            due(("mask", s), place("direct", 7), now["mask"], [("direct", s, 3, 1)])
+            due(("mask", s), ORDER["direct"][0][2 + 2 * s], now["mask"])
         for j in units:
             due(("split_q", s, j), place("split_q", j), call(now["split_q"], j),
                 [("bc", s, j, i, hop) for i in units for hop in hops] + [("handed", s, j)])

time: 153 us -> 153 us (level)
  no operation moved by 1% of the time
where the time goes in v6:
time: 153 us; the launch traced here: 151 us
  Pallas kernels  150 us (98%)
    pallas_call x1, Pallas kernels, per_device(): pl.pallas_call(body, out_shape=(jax.ShapeDtypeStruct((2, SLAB, BLK), F32)...  147 us

profile of v6, /device:TPU:37, one launch (start us, length us, event | category | flops | bytes accessed | tf_op | source)
XLA Modules:
  0.0 150.6 jit_solution(10886871173654974116)
XLA Ops:
  0.6 146.9 %purify.1 = (f32[2,128,1024]{2,1,0:T(8,128)}, f32[8,128]{1,0:T(8,128)}, f32[16,128]{1,0:T(8,128)}) custom-call(f32[1024,256]{1,0:T(8,128)} %dens.1, s32[4,16]{1,0:T(4,128)} %bitcast.1, s32[3]{0:T(128)} %br.1), custom_call_target="tpu_custom_call" | custom-call | tf_op jit(solution)/shard_map/purify/pallas_call | solution.py:496
  147.5 3.0 %place.1 = (f32[1024,256]{1,0:T(8,128)}, f32[3]{0:T(128)}) custom-call(f32[2,128,1024]{2,1,0:T(8,128)} %get-tuple-element.5.fin, f32[16,128]{1,0:T(8,128)} %get-tuple-element.6.pat, f32[8,128]{1,0:T(8,128)} %get-tuple-element.7.totals), custom_call_target="tpu_custom_call" | custom-call | tf_op jit(solution)/shard_map/place/pallas_call | solution.py:536
